TPU v7x, 128 devices: a whole 4x4x4 slice. The times are simulated.
128 devices in a mesh: flow: 32 (over y, x, core), cross: 4 (over z).
Axes of the slice: x: 4, y: 4, z: 4, core: 2. Of those that a mesh axis runs over, the one named last changes fastest.
Arguments:
- fluid_pop: float32 [384, 19, 4096], P(('flow', 'cross'))
- heat_pop: float32 [384, 7, 4096], P(('flow', 'cross'))
- solid_temp: float32 [256, 4096], P(('flow', 'cross'))
- material: int32 [256, 4096], P(('flow', 'cross')), may hold values from 0 to 7
- conductivity: float32 [8], replicated, may hold values from 0.1 to 2
- fluid_nbr: int32 [384, 18], P(('flow', 'cross')), may hold values from -1 to 383, as said below
- solid_face: int32 [384, 6], P(('flow', 'cross')), may hold values from -1 to 255, as said below
- solid_nbr: int32 [256, 6], P(('flow', 'cross')), may hold values from -1 to 255, as said below
- solid_fluid: int32 [256, 6], P(('flow', 'cross')), may hold values from -1 to 383, as said below
Outputs:
- fluid_out: float32 [384, 19, 4096], P(('flow', 'cross'))
- heat_out: float32 [384, 7, 4096], P(('flow', 'cross'))
- solid_out: float32 [256, 4096], P(('flow', 'cross'))
Inputs may be any that keep to these rules, and one draw needn't show every extreme that they name: `fluid_nbr`: the blocks tile a lattice of 32 x 4 x 5 block positions. Fluid block b is held by device b // 3 and solid block s by device s // 2, devices counted along flow, then cross; each device's blocks fill its own region of 1 x 1 x 5 positions, with 3 fluid and 2 solid blocks in ascending position order, so every neighbour of a block is held by a device whose flow and cross indices differ by at most one from its own. Entry [b, n] is the fluid block at b's position plus c_(n+1), or -1 where that position is solid or outside the lattice. `solid_face`: entry [b, k] is the solid block at fluid block b's position plus c_(k+1), or -1. `solid_nbr`: entry [s, k] is the solid block at solid block s's position plus c_(k+1), or -1. `solid_fluid`: entry [s, k] is the fluid block at solid block s's position plus c_(k+1), or -1; it is b exactly when solid_face holds s for b in the opposite direction.
All inputs are finite; a program needn't handle non-finite values.
Results may differ from a plain program's by a relative error of at most 0.0003.
Values sent between devices are 32-bit elements; how exact they have to be, the bound alone decides.
A program may use at most 192 MiB of HBM per device.

v0:
```python
import functools

import jax
import jax.numpy as jnp
from jax import lax
from jax.experimental import pallas as pl
from jax.experimental.pallas import tpu as pltpu
from jax.sharding import PartitionSpec as P

MESH = pl.DeviceIdType.MESH
F32 = jnp.float32
E = 16
W = 256
H = 128
FB = 3
SB = 2
C = [
    (0, 0, 0),
    (1, 0, 0),
    (-1, 0, 0),
    (0, 1, 0),
    (0, -1, 0),
    (0, 0, 1),
    (0, 0, -1),
    (1, 1, 0),
    (-1, -1, 0),
    (1, -1, 0),
    (-1, 1, 0),
    (1, 0, 1),
    (-1, 0, -1),
    (1, 0, -1),
    (-1, 0, 1),
    (0, 1, 1),
    (0, -1, -1),
    (0, 1, -1),
    (0, -1, 1),
]
OPP = [0, 2, 1, 4, 3, 6, 5, 8, 7, 10, 9, 12, 11, 14, 13, 16, 15, 18, 17]
PX = ([1, 7, 9, 11, 13], [2, 8, 10, 12, 14])
PY = ([3, 7, 10, 15, 17], [4, 8, 9, 16, 18])
HEAT = 5
SIDES = [(1, 0), (-1, 0), (0, 1), (0, -1)]
CORNERS = [(1, 1), (1, -1), (-1, -1), (-1, 1)]
PEERS = SIDES + CORNERS
CORNER_SRC = [(0, 1, 1), (0, 2, 0), (1, 1, 0), (1, 2, 1)]
CORNER_OF = {7: 0, 9: 1, 8: 2, 10: 3}
N_COPY = 20


def lroll(v, s):
    n = v.shape[1]
    s = s % n
    return v if s == 0 else pltpu.roll(v, s, axis=1)


def rroll(v, s):
    n = v.shape[0]
    s = s % n
    return v if s == 0 else pltpu.roll(v, s, axis=0)


def lanes(shape):
    return lax.broadcasted_iota(jnp.int32, shape, 1)


def rows(shape):
    return lax.broadcasted_iota(jnp.int32, shape, 0)


def collide_tile(G, Q, b, rs, ls):
    def ld(p):
        return G[b, p, rs, ls]

    f = [ld(p) for p in range(19)]
    d = [None] * 19
    for p in (1, 3, 5, 7, 9, 11, 13, 15, 17):
        d[p] = f[p] - f[p + 1]
    s1 = ((f[1] + f[2]) + (f[3] + f[4])) + (f[5] + f[6])
    s2 = (((f[7] + f[8]) + (f[9] + f[10])) + ((f[11] + f[12]) + (f[13] + f[14]))) + (
        (f[15] + f[16]) + (f[17] + f[18])
    )
    rho = f[0] * (1.0 / 3.0) + s1 * (1.0 / 18.0) + s2 * (1.0 / 36.0)
    jx = d[1] * (1.0 / 18.0) + ((d[7] + d[9]) + (d[11] + d[13])) * (1.0 / 36.0)
    jy = d[3] * (1.0 / 18.0) + ((d[7] - d[9]) + (d[15] + d[17])) * (1.0 / 36.0)
    jz = d[5] * (1.0 / 18.0) + ((d[11] - d[13]) + (d[15] - d[17])) * (1.0 / 36.0)
    inv = 1.0 / rho
    u = (jx * inv, jy * inv, jz * inv)
    j = (jx, jy, jz)
    base = 1.25 * rho - 1.875 * (jx * u[0] + jy * u[1] + jz * u[2])
    G[b, 0, rs, ls] = base - 0.25 * f[0]
    cus = {}
    for p in (1, 3, 5, 7, 9, 11, 13, 15, 17):
        cj = None
        cu = None
        for a in range(3):
            s = C[p][a]
            if s == 0:
                continue
            if cj is None:
                cj, cu = j[a], u[a]
            elif s > 0:
                cj, cu = cj + j[a], cu + u[a]
            else:
                cj, cu = cj - j[a], cu - u[a]
        even = base + 5.625 * (cj * cu)
        odd = 3.75 * cj
        G[b, p, rs, ls] = (even + odd) - 0.25 * f[p]
        G[b, p + 1, rs, ls] = (even - odd) - 0.25 * f[p + 1]
        cus[p] = cu
    h = [Q[b, k, rs, ls] for k in range(7)]
    hs = ((h[1] + h[2]) + (h[3] + h[4])) + (h[5] + h[6])
    t11 = (h[0] * 0.25 + hs * 0.125) * 1.1
    t44 = 4.0 * t11
    Q[b, 0, rs, ls] = t11 - 0.1 * h[0]
    for k in (1, 3, 5):
        o = t44 * cus[k]
        Q[b, k, rs, ls] = (t11 + o) - 0.1 * h[k]
        Q[b, k + 1, rs, ls] = (t11 - o) - 0.1 * h[k + 1]


def kernel(
    nf,
    nc,
    fluid_in,
    heat_in,
    temp_in,
    mat_in,
    cond,
    nbr,
    wall,
    snbr,
    sflu,
    fluid_out,
    heat_out,
    solid_out,
    G,
    Q,
    GO,
    QO,
    T,
    M,
    KAP,
    TO,
    XS,
    XR,
    YS,
    YR,
    CR,
    XTS,
    XTR,
    YTS,
    YTR,
    DXS,
    DXR,
    DYS,
    DYR,
    in_sem,
    out_sem,
    send_sem,
    recv_sem,
):
    fl = lax.axis_index("flow")
    cr = lax.axis_index("cross")

    def peer(df, dc):
        return (lax.rem(fl + (df + nf), nf), lax.rem(cr + (dc + nc), nc))

    barrier = pltpu.get_barrier_semaphore()
    for df, dc in PEERS:
        pl.semaphore_signal(barrier, inc=1, device_id=peer(df, dc), device_id_type=MESH)

    def load(src, dst, sem):
        for x in range(E):
            pltpu.make_async_copy(
                src.at[..., pl.ds(W * x, W)], dst.at[..., x, :], sem
            ).start()

    def all_of(ref, sem):
        return pltpu.make_async_copy(ref, ref, sem)

    load(temp_in, T, in_sem.at[0])
    load(mat_in, M, in_sem.at[1])
    for b in range(FB):
        load(fluid_in.at[b], G.at[b], in_sem.at[2 + 2 * b])
        load(heat_in.at[b], Q.at[b], in_sem.at[3 + 2 * b])

    copies = {}

    def send(i, src, dst, df, dc):
        copies[i] = pltpu.make_async_remote_copy(
            src_ref=src,
            dst_ref=dst,
            send_sem=send_sem.at[i],
            recv_sem=recv_sem.at[i],
            device_id=peer(df, dc),
            device_id_type=MESH,
        )
        copies[i].start()

    wide = (E, W)
    lw = lanes(wide)
    rw = rows(wide)
    zw = jnp.bitwise_and(lw, E - 1)
    lh = lanes((E, H))
    group = jnp.right_shift(lh, 4)

    def base_of(df, dc):
        return (fl + df) * nc + (cr + dc)

    all_of(T, in_sem.at[0]).wait()
    all_of(M, in_sem.at[1]).wait()
    for s in range(SB):
        m = M[s]
        k = jnp.full(wide, cond[0], F32)
        for i in range(1, 8):
            k = jnp.where(m == i, cond[i], k)
        KAP[s] = k

    def pack_y(pieces, side):
        acc = None
        for g, v in enumerate(pieces):
            if side == 0:
                r = lroll(v[:, H:], E * g - (H - E))
            else:
                r = lroll(v[:, :H], E * g)
            acc = r if acc is None else jnp.where(group == g, r, acc)
        return acc

    for side in range(2):
        x = E - 1 if side == 0 else 0
        for s in range(SB):
            XTS[side, s, 0:1, :] = T[s, x : x + 1, :]
            XTS[side, s, 1:2, :] = KAP[s, x : x + 1, :]
        YTS[side] = pack_y([T[0], KAP[0], T[1], KAP[1]], side)

    pl.semaphore_wait(barrier, len(PEERS))
    for i, (df, dc) in enumerate(SIDES):
        side = i % 2
        if i < 2:
            send(i, XTS.at[side], XTR.at[side], df, dc)
        else:
            send(i, YTS.at[side], YTR.at[side], df, dc)

    for b in range(FB):
        all_of(G.at[b], in_sem.at[2 + 2 * b]).wait()
        all_of(Q.at[b], in_sem.at[3 + 2 * b]).wait()
        for xh in range(2):
            for yh in range(2):
                collide_tile(G, Q, b, pl.ds(8 * xh, 8), pl.ds(H * yh, H))
        for side in range(2):
            x = E - 1 if side == 0 else 0
            for r in range(5):
                XS[side, b, r : r + 1, :] = G[b, PX[side][r], x : x + 1, :]
            XS[side, b, HEAT : HEAT + 1, :] = Q[b, 1 + side, x : x + 1, :]
            YS[side, b] = pack_y(
                [G[b, PY[side][r]] for r in range(5)] + [Q[b, 3 + side]], side
            )

    for i, (df, dc) in enumerate(SIDES):
        side = i % 2
        if i < 2:
            send(4 + i, XS.at[side], XR.at[side], df, dc)
        else:
            send(4 + i, YS.at[side], YR.at[side], df, dc)
    for i, (df, dc) in enumerate(CORNERS):
        side, r, half = CORNER_SRC[i]
        send(
            8 + i,
            XS.at[side, :, pl.ds(r, 1), pl.ds(H * half, H)],
            CR.at[i],
            df,
            dc,
        )

    def slot(idv, base, n):
        return jnp.clip(idv - base * n, 0, n - 1)

    def unpack_group(v, g, lo):
        return lroll(v, -E * g) if lo else lroll(v, (H - E) - E * g)

    def widen(v, lo):
        return jnp.concatenate([v, v], axis=1)

    def pick(sel, a, b_):
        return jnp.where(jnp.full(a.shape, sel) == 0, a, b_)

    edges = [rw == E - 1, rw == 0, lw >= W - E, lw < E, zw == E - 1, zw == 0]

    def shifted(v, k):
        return [
            lambda: rroll(v, -1),
            lambda: rroll(v, 1),
            lambda: lroll(v, -E),
            lambda: lroll(v, E),
            lambda: lroll(v, -1),
            lambda: lroll(v, 1),
        ][k]()

    def step_base(k):
        return base_of(C[k + 1][0], C[k + 1][1])

    def z_ghost(v, k):
        return lroll(v, E - 1) if k == 4 else lroll(v, 1 - E)

    def solid_ghost(k, s, sl, q, field):
        if k < 2:
            return XTR[1 - k, sl, q : q + 1, :]
        if k < 4:
            v = YTR[1 - (k - 2)]
            lo = k == 3
            return widen(pick(sl, unpack_group(v, q, lo), unpack_group(v, 2 + q, lo)), lo)
        return z_ghost(field[1 - s], k)

    def heat_ghost(k, fsl):
        if k < 2:
            return XR[1 - k, fsl, HEAT : HEAT + 1, :]
        if k < 4:
            lo = k == 3
            return widen(unpack_group(YR[1 - (k - 2), fsl], HEAT, lo), lo)
        return z_ghost(Q[fsl, 6 if k == 4 else 5], k)

    for i in range(12):
        copies[i].wait_recv()

    kmax = cond[0]
    for i in range(1, 8):
        kmax = jnp.maximum(kmax, cond[i])
    radius = jnp.full((8, H), kmax * 6.0, F32)
    center = radius + 1.0
    sigma = center / radius

    def grow(v):
        v = jnp.concatenate([v, v], axis=0)
        return jnp.concatenate([v, v], axis=1)

    inv_center = grow(1.0 / center)
    rho0 = 1.0 / sigma
    rho1 = 1.0 / (2.0 * sigma - rho0)
    rho2 = 1.0 / (2.0 * sigma - rho1)
    coef = [
        (grow(rho1 * rho0), grow(2.0 * rho1 / radius)),
        (grow(rho2 * rho1), grow(2.0 * rho2 / radius)),
    ]

    sid = [[snbr[s, k] for k in range(6)] for s in range(SB)]
    fid = [[sflu[s, k] for k in range(6)] for s in range(SB)]
    ssl = [[slot(sid[s][k], step_base(k), SB) for k in range(6)] for s in range(SB)]
    links = []
    resid = []
    upd = []
    sol = []
    for s in range(SB):
        t = T[s]
        kap = KAP[s]
        acc = jnp.zeros(wide, F32)
        row = []
        for k in range(6):
            sl = ssl[s][k]
            live = jnp.full(wide, sid[s][k]) >= 0
            wet = jnp.full(wide, fid[s][k]) >= 0
            kb = jnp.where(edges[k], solid_ghost(k, s, sl, 1, KAP), shifted(kap, k))
            link = (2.0 * kap * kb) / (kap + kb)
            link = jnp.where(edges[k] & ~live, 0.0, link)
            row.append(link)
            tb = jnp.where(edges[k], solid_ghost(k, s, sl, 0, T), shifted(t, k))
            hb = heat_ghost(k, slot(fid[s][k], step_base(k), FB))
            wet_edge = edges[k] & wet
            acc = acc + jnp.where(wet_edge, 1.0, link) * (jnp.where(wet_edge, hb, tb) - t)
        links.append(row)
        d = acc * inv_center
        resid.append(acc)
        upd.append(d)
        sol.append(t + d)

    def share(n):
        for side in range(2):
            x = E - 1 if side == 0 else 0
            for s in range(SB):
                DXS[n, side, s : s + 1, :] = upd[s][x : x + 1, :]
            DYS[n, side] = pack_y(upd, side)
        for i, (df, dc) in enumerate(SIDES):
            side = i % 2
            if i < 2:
                send(12 + 4 * n + i, DXS.at[n, side], DXR.at[n, side], df, dc)
            else:
                send(12 + 4 * n + i, DYS.at[n, side], DYR.at[n, side], df, dc)

    def update_ghost(n, k, s, sl):
        if k < 2:
            v = DXR[n, 1 - k]
            return pick(sl, v[0:1], v[1:2])
        if k < 4:
            v = DYR[n, 1 - (k - 2)]
            lo = k == 3
            return widen(pick(sl, unpack_group(v, 0, lo), unpack_group(v, 1, lo)), lo)
        return z_ghost(upd[1 - s], k)

    def sweep(n):
        for i in range(4):
            copies[12 + 4 * n + i].wait_recv()
        fresh = []
        for s in range(SB):
            d = upd[s]
            acc = d
            for k in range(6):
                db = jnp.where(edges[k], update_ghost(n, k, s, ssl[s][k]), shifted(d, k))
                acc = acc + links[s][k] * (d - db)
            resid[s] = resid[s] - acc
            nd = coef[n][0] * d + coef[n][1] * resid[s]
            fresh.append(nd)
            sol[s] = sol[s] + nd
        for s in range(SB):
            upd[s] = fresh[s]

    share(0)

    def x_face(b, side):
        shape = (8, W)
        r8 = rows(shape)
        l8 = lanes(shape)
        z8 = jnp.bitwise_and(l8, E - 1)
        df = -1 if side == 0 else 1
        dirn = 2 if side == 0 else 1
        bf = base_of(df, 0)
        main_id = nbr[b, dirn - 1]
        a = XR[side, slot(main_id, bf, FB)]
        val = a
        ids = jnp.full(shape, main_id)
        for r, p in enumerate(PX[side]):
            _, cy, cz = C[p]
            if r == 0:
                continue
            src = OPP[p]
            cid = nbr[b, src - 1]
            if cy:
                corner = CR[CORNER_OF[p], slot(cid, base_of(df, -cy), FB)]
                corner = jnp.broadcast_to(corner, (8, H))
                corner = lroll(corner, E * cy)
                corner = jnp.concatenate([corner, corner], axis=1)
                edge = l8 < E if cy > 0 else l8 >= W - E
                cand = jnp.where(edge, corner, lroll(a, E * cy))
            else:
                other = XR[side, slot(cid, bf, FB)]
                edge = z8 == 0 if cz > 0 else z8 == E - 1
                cand = jnp.where(edge, lroll(other, -(E - 1) * cz), lroll(a, cz))
            val = jnp.where(r8 == r, cand, val)
            ids = jnp.where((r8 == r) & edge, jnp.full(shape, cid), ids)
        fall = XS[1 - side, b]
        wid = wall[b, dirn - 1]
        tw = XTR[side, slot(wid, bf, SB), 0:1, :]
        hot = (r8 == HEAT) & (jnp.full(shape, wid) >= 0)
        fall = jnp.where(hot, 2.0 * tw - fall, fall)
        return jnp.where(ids >= 0, val, fall)

    def y_face(b, side):
        shape = (E, H)
        zh = jnp.bitwise_and(lh, E - 1)
        dc = -1 if side == 0 else 1
        dirn = 4 if side == 0 else 3
        bf = base_of(0, dc)
        main_id = nbr[b, dirn - 1]
        a = YR[side, slot(main_id, bf, FB)]
        val = a
        ids = jnp.full(shape, main_id)
        for r, p in enumerate(PY[side]):
            cx, _, cz = C[p]
            if r == 0:
                continue
            if cx:
                val = jnp.where(group == r, rroll(a, cx), val)
                continue
            cid = nbr[b, OPP[p] - 1]
            other = YR[side, slot(cid, bf, FB)]
            edge = zh == 0 if cz > 0 else zh == E - 1
            cand = jnp.where(edge, lroll(other, -(E - 1) * cz), lroll(a, cz))
            val = jnp.where(group == r, cand, val)
            ids = jnp.where((group == r) & edge, jnp.full(shape, cid), ids)
        fall = YS[1 - side, b]
        wid = wall[b, dirn - 1]
        wsl = slot(wid, bf, SB)
        tv = YTR[side]
        tw = pick(wsl, lroll(tv, E * HEAT), lroll(tv, E * (HEAT - 2)))
        hot = (group == HEAT) & (jnp.full(shape, wid) >= 0)
        fall = jnp.where(hot, 2.0 * tw - fall, fall)
        return jnp.where(ids >= 0, val, fall)

    def stream(b):
        yf = [y_face(b, 0), y_face(b, 1)]

        def main(ref, p, q):
            cx, cy, cz = C[p]
            s = E * cy + cz
            out = lroll(rroll(ref[b, p], cx), s)
            if cz:
                back = ref[b, OPP[p]]
                adj = (b - cz) % FB
                if 0 <= b - cz < FB:
                    other = lroll(rroll(ref[adj, p], cx), E * cy - (E - 1) * cz)
                    zid = nbr[b, (6 if cz > 0 else 5) - 1]
                else:
                    other = None
                if ref is Q:
                    wid = wall[b, (6 if cz > 0 else 5) - 1]
                    tw = lroll(T[slot(wid, base_of(0, 0), SB)], -(E - 1) * cz)
                    back = jnp.where(jnp.full(wide, wid) >= 0, 2.0 * tw - back, back)
                if other is not None:
                    back = jnp.where(jnp.full(wide, zid) >= 0, other, back)
                edge = zw == 0 if cz > 0 else zw == E - 1
                out = jnp.where(edge, back, out)
            if cy:
                lo = cy > 0
                v = unpack_group(yf[0 if lo else 1], q, lo)
                if lo:
                    out = jnp.concatenate(
                        [jnp.where(lh < E, v, out[:, :H]), out[:, H:]], axis=1
                    )
                else:
                    out = jnp.concatenate(
                        [out[:, :H], jnp.where(lh >= H - E, v, out[:, H:])], axis=1
                    )
            return out

        GO[b, 0] = G[b, 0]
        QO[b, 0] = Q[b, 0]
        for p in range(1, 19):
            cy = C[p][1]
            q = PY[0 if cy > 0 else 1].index(p) if cy else None
            GO[b, p] = main(G, p, q)
        for p in range(1, 7):
            QO[b, p] = main(Q, p, HEAT)
        for side in range(2):
            xf = x_face(b, side)
            x = 0 if side == 0 else E - 1
            for r, p in enumerate(PX[side]):
                GO[b, p, x : x + 1, :] = xf[r : r + 1]
            QO[b, 1 + side, x : x + 1, :] = xf[HEAT : HEAT + 1]

    def put(src, dst, sem):
        for x in range(E):
            pltpu.make_async_copy(
                src.at[..., x, :], dst.at[..., pl.ds(W * x, W)], sem
            ).start()

    def finish(b):
        stream(b)
        put(GO.at[b], fluid_out.at[b], out_sem.at[2 * b])
        put(QO.at[b], heat_out.at[b], out_sem.at[2 * b + 1])

    finish(0)
    sweep(0)
    share(1)
    finish(1)
    sweep(1)
    for s in range(SB):
        TO[s] = sol[s]
    put(TO, solid_out, out_sem.at[6])
    finish(2)

    for b in range(FB):
        all_of(GO.at[b], out_sem.at[2 * b]).wait()
        all_of(QO.at[b], out_sem.at[2 * b + 1]).wait()
    all_of(TO, out_sem.at[6]).wait()
    for i in range(N_COPY):
        copies[i].wait_send()


def body(nf, nc, fluid_pop, heat_pop, solid_temp, material, cond, nbr, wall, snbr, sflu):
    hbm = pl.BlockSpec(memory_space=pl.ANY)
    smem = pl.BlockSpec(memory_space=pltpu.SMEM)

    def vm(*shape):
        return pltpu.VMEM(shape, F32)

    return pl.pallas_call(
        functools.partial(kernel, nf, nc),
        out_shape=(
            jax.ShapeDtypeStruct(fluid_pop.shape, F32),
            jax.ShapeDtypeStruct(heat_pop.shape, F32),
            jax.ShapeDtypeStruct(solid_temp.shape, F32),
        ),
        in_specs=[hbm] * 4 + [smem] * 5,
        out_specs=(hbm, hbm, hbm),
        scratch_shapes=[
            vm(FB, 19, E, W),
            vm(FB, 7, E, W),
            vm(FB, 19, E, W),
            vm(FB, 7, E, W),
            vm(SB, E, W),
            pltpu.VMEM((SB, E, W), jnp.int32),
            vm(SB, E, W),
            vm(SB, E, W),
            vm(2, FB, 8, W),
            vm(2, FB, 8, W),
            vm(2, FB, E, H),
            vm(2, FB, E, H),
            vm(4, FB, 1, H),
            vm(2, SB, 2, W),
            vm(2, SB, 2, W),
            vm(2, E, H),
            vm(2, E, H),
            vm(2, 2, SB, W),
            vm(2, 2, SB, W),
            vm(2, 2, E, H),
            vm(2, 2, E, H),
            pltpu.SemaphoreType.DMA((8,)),
            pltpu.SemaphoreType.DMA((7,)),
            pltpu.SemaphoreType.DMA((N_COPY,)),
            pltpu.SemaphoreType.DMA((N_COPY,)),
        ],
        compiler_params=pltpu.CompilerParams(
            collective_id=0, has_side_effects=True, vmem_limit_bytes=32 * 1024 * 1024
        ),
    )(fluid_pop, heat_pop, solid_temp, material, cond, nbr, wall, snbr, sflu)


def solution(mesh):
    both = ("flow", "cross")
    in_specs = (
        P(both, None, None),
        P(both, None, None),
        P(both, None),
        P(both, None),
        P(),
        P(both, None),
        P(both, None),
        P(both, None),
        P(both, None),
    )
    out_specs = (P(both, None, None), P(both, None, None), P(both, None))
    return jax.shard_map(
        functools.partial(body, mesh.shape["flow"], mesh.shape["cross"]),
        mesh=mesh,
        in_specs=in_specs,
        out_specs=out_specs,
        check_vma=False,
    )
```

profile of v0, /device:TPU:0, one launch (start us, length us, event | category | flops | bytes accessed | tf_op | source)
XLA Modules:
  0.0 33.7 jit_solution(5079254032765212658)
XLA Ops:
  0.6 0.0 copy-start
  0.6 1.3 %copy-done = f32[3,19,4096]{2,1,0:T(8,128)S(1)} copy-done((f32[3,19,4096]{2,1,0:T(8,128)S(1)}, f32[3,19,4096]{2,1,0:T(8,128)}, u32[]{:S(2)}) %copy-start) | copy-done | bytes 933912
  1.9 0.0 copy-start.1
  1.9 1.0 %copy-done.1 = f32[3,7,4096]{2,1,0:T(8,128)S(1)} copy-done((f32[3,7,4096]{2,1,0:T(8,128)S(1)}, f32[3,7,4096]{2,1,0:T(8,128)}, u32[]{:S(2)}) %copy-start.1) | copy-done | bytes 344088
  2.9 0.0 copy-start.2
  2.9 0.8 %copy-done.2 = f32[2,4096]{1,0:T(2,128)S(1)} copy-done((f32[2,4096]{1,0:T(2,128)S(1)}, f32[2,4096]{1,0:T(2,128)}, u32[]{:S(2)}) %copy-start.2) | copy-done | bytes 32792
  3.7 0.0 copy-start.3
  3.7 0.8 %copy-done.3 = s32[2,4096]{1,0:T(2,128)S(1)} copy-done((s32[2,4096]{1,0:T(2,128)S(1)}, s32[2,4096]{1,0:T(2,128)}, u32[]{:S(2)}) %copy-start.3) | copy-done | bytes 32792
  4.4 0.0 copy-start.4
  4.4 0.7 %copy-done.4 = s32[3,18]{1,0:T(4,128)S(1)} copy-done((s32[3,18]{1,0:T(4,128)S(1)}, s32[3,18]{1,0:T(4,128)}, u32[]{:S(2)}) %copy-start.4) | copy-done | bytes 240
  5.1 0.0 copy-start.5
  5.1 0.7 %copy-done.5 = s32[3,6]{1,0:T(4,128)S(1)} copy-done((s32[3,6]{1,0:T(4,128)S(1)}, s32[3,6]{1,0:T(4,128)}, u32[]{:S(2)}) %copy-start.5) | copy-done | bytes 96
  5.8 0.0 copy-start.6
  5.8 0.7 %copy-done.6 = s32[2,6]{1,0:T(2,128)S(1)} copy-done((s32[2,6]{1,0:T(2,128)S(1)}, s32[2,6]{1,0:T(2,128)}, u32[]{:S(2)}) %copy-start.6) | copy-done | bytes 72
  6.5 0.0 copy-start.7
  6.5 0.7 %copy-done.7 = s32[2,6]{1,0:T(2,128)S(1)} copy-done((s32[2,6]{1,0:T(2,128)S(1)}, s32[2,6]{1,0:T(2,128)}, u32[]{:S(2)}) %copy-start.7) | copy-done | bytes 72
  7.1 0.0 copy-start.8
  7.1 0.7 %copy-done.8 = f32[8]{0:T(128)S(1)} copy-done((f32[8]{0:T(128)S(1)}, f32[8]{0:T(128)}, u32[]{:S(2)}) %copy-start.8) | copy-done | bytes 56
  7.8 23.5 %shard_map.112 = (f32[3,19,4096]{2,1,0:T(8,128)S(1)}, f32[3,7,4096]{2,1,0:T(8,128)S(1)}, f32[2,4096]{1,0:T(2,128)S(1)}) custom-call(f32[3,19,4096]{2,1,0:T(8,128)S(1)} %copy-done, f32[3,7,4096]{2,1,0:T(8,128)S(1)} %copy-done.1, f32[2,4096]{1,0:T(2,128)S(1)} %copy-done.2, s32[2,4096]{1,0:T(2,128)S(1)} %copy-done.3, f32[8]{0:T(128)S(1)} %copy-done.8, ...), custom_call_target="tpu_custom_call" | custom-call | tf_op jit(solution)/shard_map/pallas_call | solution.py:574
  31.3 1.0 %copy.15 = f32[3,19,4096]{2,1,0:T(8,128)} copy(f32[3,19,4096]{2,1,0:T(8,128)S(1)} %get-tuple-element.6) | data formatting | bytes 1867776
  32.3 0.7 %copy.16 = f32[3,7,4096]{2,1,0:T(8,128)} copy(f32[3,7,4096]{2,1,0:T(8,128)S(1)} %get-tuple-element.7) | data formatting | bytes 688128
  33.1 0.6 %copy.17 = f32[2,4096]{1,0:T(2,128)} copy(f32[2,4096]{1,0:T(2,128)S(1)} %get-tuple-element.8) | data formatting | bytes 65536
Async XLA Ops:
  0.6 1.3 %copy-start = (f32[3,19,4096]{2,1,0:T(8,128)S(1)}, f32[3,19,4096]{2,1,0:T(8,128)}, u32[]{:S(2)}) copy-start(f32[3,19,4096]{2,1,0:T(8,128)} %fluid_in.1) | copy-start | bytes 2801668
  1.9 1.0 %copy-start.1 = (f32[3,7,4096]{2,1,0:T(8,128)S(1)}, f32[3,7,4096]{2,1,0:T(8,128)}, u32[]{:S(2)}) copy-start(f32[3,7,4096]{2,1,0:T(8,128)} %heat_in.1) | copy-start | bytes 1032196
  2.9 0.8 %copy-start.2 = (f32[2,4096]{1,0:T(2,128)S(1)}, f32[2,4096]{1,0:T(2,128)}, u32[]{:S(2)}) copy-start(f32[2,4096]{1,0:T(2,128)} %temp_in.1) | copy-start | bytes 98308
  3.7 0.8 %copy-start.3 = (s32[2,4096]{1,0:T(2,128)S(1)}, s32[2,4096]{1,0:T(2,128)}, u32[]{:S(2)}) copy-start(s32[2,4096]{1,0:T(2,128)} %mat_in.1) | copy-start | bytes 98308
  4.4 0.7 %copy-start.4 = (s32[3,18]{1,0:T(4,128)S(1)}, s32[3,18]{1,0:T(4,128)}, u32[]{:S(2)}) copy-start(s32[3,18]{1,0:T(4,128)} %nbr.1) | copy-start | bytes 652
  5.1 0.7 %copy-start.5 = (s32[3,6]{1,0:T(4,128)S(1)}, s32[3,6]{1,0:T(4,128)}, u32[]{:S(2)}) copy-start(s32[3,6]{1,0:T(4,128)} %wall.1) | copy-start | bytes 220
  5.8 0.7 %copy-start.6 = (s32[2,6]{1,0:T(2,128)S(1)}, s32[2,6]{1,0:T(2,128)}, u32[]{:S(2)}) copy-start(s32[2,6]{1,0:T(2,128)} %snbr.1) | copy-start | bytes 148
  6.5 0.7 %copy-start.7 = (s32[2,6]{1,0:T(2,128)S(1)}, s32[2,6]{1,0:T(2,128)}, u32[]{:S(2)}) copy-start(s32[2,6]{1,0:T(2,128)} %sflu.1) | copy-start | bytes 148
  7.1 0.7 %copy-start.8 = (f32[8]{0:T(128)S(1)}, f32[8]{0:T(128)}, u32[]{:S(2)}) copy-start(f32[8]{0:T(128)} %cond.1) | copy-start | bytes 100
where the time goes:
time: 34.1 us; the launch traced here: 33.7 us
  Pallas kernels  23.5 us (69%)
  local copies, waits for them, and re-layouts  9.52 us (28%)
  between operations  0.66 us (2%)
    pallas_call x1, Pallas kernels, body(): pl.pallas_call(functools.partial(kernel, nf, nc), out_shape=(jax.ShapeDty...  23.5 us
    unnamed x21, local copies, waits for them, and re-layouts  9.52 us

commit v1 on v0

--- a/solution.py
+++ b/solution.py
@@ -125,11 +125,11 @@
     heat_in,
     temp_in,
     mat_in,
-    cond,
-    nbr,
-    wall,
-    snbr,
-    sflu,
+    cond_in,
+    nbr_in,
+    wall_in,
+    snbr_in,
+    sflu_in,
     fluid_out,
     heat_out,
     solid_out,
@@ -154,6 +154,11 @@
     DXR,
     DYS,
     DYR,
+    cond,
+    nbr,
+    wall,
+    snbr,
+    sflu,
     in_sem,
     out_sem,
     send_sem,
@@ -162,12 +167,26 @@
     fl = lax.axis_index("flow")
     cr = lax.axis_index("cross")
 
-    def peer(df, dc):
-        return (lax.rem(fl + (df + nf), nf), lax.rem(cr + (dc + nc), nc))
+    inside = {-1: (fl > 0, cr > 0), 0: (True, True), 1: (fl < nf - 1, cr < nc - 1)}
+
+    def near(df, dc):
+        a, b = inside[df][0], inside[dc][1]
+        if df == 0:
+            return b
+        return a if dc == 0 else jnp.logical_and(a, b)
 
     barrier = pltpu.get_barrier_semaphore()
     for df, dc in PEERS:
-        pl.semaphore_signal(barrier, inc=1, device_id=peer(df, dc), device_id_type=MESH)
+
+        @pl.when(near(df, dc))
+        def _():
+            pl.semaphore_signal(
+                barrier, inc=1, device_id=(fl + df, cr + dc), device_id_type=MESH
+            )
+
+    nx = 2 - (fl == 0).astype(jnp.int32) - (fl == nf - 1).astype(jnp.int32)
+    ny = 2 - (cr == 0).astype(jnp.int32) - (cr == nc - 1).astype(jnp.int32)
+    n_peers = nx + ny + nx * ny
 
     def load(src, dst, sem):
         for x in range(E):
@@ -178,6 +197,16 @@
     def all_of(ref, sem):
         return pltpu.make_async_copy(ref, ref, sem)
 
+    tables = [
+        (cond_in, cond, 8),
+        (nbr_in, nbr, 9),
+        (wall_in, wall, 10),
+        (snbr_in, snbr, 11),
+        (sflu_in, sflu, 12),
+    ]
+    tables = [pltpu.make_async_copy(a, b, in_sem.at[i]) for a, b, i in tables]
+    for c in tables:
+        c.start()
     load(temp_in, T, in_sem.at[0])
     load(mat_in, M, in_sem.at[1])
     for b in range(FB):
@@ -185,6 +214,7 @@
         load(heat_in.at[b], Q.at[b], in_sem.at[3 + 2 * b])
 
     copies = {}
+    steps = {}
 
     def send(i, src, dst, df, dc):
         copies[i] = pltpu.make_async_remote_copy(
@@ -192,10 +222,19 @@
             dst_ref=dst,
             send_sem=send_sem.at[i],
             recv_sem=recv_sem.at[i],
-            device_id=peer(df, dc),
+            device_id=(fl + df, cr + dc),
             device_id_type=MESH,
         )
-        copies[i].start()
+        steps[i] = (df, dc)
+
+        @pl.when(near(df, dc))
+        def _():
+            copies[i].start()
+
+    def received(i):
+        @pl.when(near(-steps[i][0], -steps[i][1]))
+        def _():
+            copies[i].wait_recv()
 
     wide = (E, W)
     lw = lanes(wide)
@@ -207,8 +246,11 @@
     def base_of(df, dc):
         return (fl + df) * nc + (cr + dc)
 
-    all_of(T, in_sem.at[0]).wait()
-    all_of(M, in_sem.at[1]).wait()
+    with jax.named_scope("wait_solid"):
+        for c in tables:
+            c.wait()
+        all_of(T, in_sem.at[0]).wait()
+        all_of(M, in_sem.at[1]).wait()
     for s in range(SB):
         m = M[s]
         k = jnp.full(wide, cond[0], F32)
@@ -233,7 +275,8 @@
             XTS[side, s, 1:2, :] = KAP[s, x : x + 1, :]
         YTS[side] = pack_y([T[0], KAP[0], T[1], KAP[1]], side)
 
-    pl.semaphore_wait(barrier, len(PEERS))
+    with jax.named_scope("entry_barrier"):
+        pl.semaphore_wait(barrier, n_peers)
     for i, (df, dc) in enumerate(SIDES):
         side = i % 2
         if i < 2:
@@ -242,11 +285,13 @@
             send(i, YTS.at[side], YTR.at[side], df, dc)
 
     for b in range(FB):
-        all_of(G.at[b], in_sem.at[2 + 2 * b]).wait()
-        all_of(Q.at[b], in_sem.at[3 + 2 * b]).wait()
-        for xh in range(2):
-            for yh in range(2):
-                collide_tile(G, Q, b, pl.ds(8 * xh, 8), pl.ds(H * yh, H))
+        with jax.named_scope("wait_pops"):
+            all_of(G.at[b], in_sem.at[2 + 2 * b]).wait()
+            all_of(Q.at[b], in_sem.at[3 + 2 * b]).wait()
+        with jax.named_scope("collide"):
+            for xh in range(2):
+                for yh in range(2):
+                    collide_tile(G, Q, b, pl.ds(8 * xh, 8), pl.ds(H * yh, H))
         for side in range(2):
             x = E - 1 if side == 0 else 0
             for r in range(5):
@@ -319,8 +364,9 @@
             return widen(unpack_group(YR[1 - (k - 2), fsl], HEAT, lo), lo)
         return z_ghost(Q[fsl, 6 if k == 4 else 5], k)
 
-    for i in range(12):
-        copies[i].wait_recv()
+    with jax.named_scope("wait_faces"):
+        for i in range(12):
+            received(i)
 
     kmax = cond[0]
     for i in range(1, 8):
@@ -364,6 +410,7 @@
             row.append(link)
             tb = jnp.where(edges[k], solid_ghost(k, s, sl, 0, T), shifted(t, k))
             hb = heat_ghost(k, slot(fid[s][k], step_base(k), FB))
+            tb = jnp.where(edges[k] & ~live, t, tb)
             wet_edge = edges[k] & wet
             acc = acc + jnp.where(wet_edge, 1.0, link) * (jnp.where(wet_edge, hb, tb) - t)
         links.append(row)
@@ -396,14 +443,17 @@
         return z_ghost(upd[1 - s], k)
 
     def sweep(n):
-        for i in range(4):
-            copies[12 + 4 * n + i].wait_recv()
+        with jax.named_scope("wait_updates"):
+            for i in range(4):
+                received(12 + 4 * n + i)
         fresh = []
         for s in range(SB):
             d = upd[s]
             acc = d
             for k in range(6):
-                db = jnp.where(edges[k], update_ghost(n, k, s, ssl[s][k]), shifted(d, k))
+                ghost = update_ghost(n, k, s, ssl[s][k])
+                ghost = jnp.where(jnp.full(ghost.shape, sid[s][k]) >= 0, ghost, 0.0)
+                db = jnp.where(edges[k], ghost, shifted(d, k))
                 acc = acc + links[s][k] * (d - db)
             resid[s] = resid[s] - acc
             nd = coef[n][0] * d + coef[n][1] * resid[s]
@@ -542,7 +592,8 @@
             ).start()
 
     def finish(b):
-        stream(b)
+        with jax.named_scope("stream"):
+            stream(b)
         put(GO.at[b], fluid_out.at[b], out_sem.at[2 * b])
         put(QO.at[b], heat_out.at[b], out_sem.at[2 * b + 1])
 
@@ -556,17 +607,20 @@
     put(TO, solid_out, out_sem.at[6])
     finish(2)
 
-    for b in range(FB):
-        all_of(GO.at[b], out_sem.at[2 * b]).wait()
-        all_of(QO.at[b], out_sem.at[2 * b + 1]).wait()
-    all_of(TO, out_sem.at[6]).wait()
+    with jax.named_scope("wait_stores"):
+        for b in range(FB):
+            all_of(GO.at[b], out_sem.at[2 * b]).wait()
+            all_of(QO.at[b], out_sem.at[2 * b + 1]).wait()
+        all_of(TO, out_sem.at[6]).wait()
     for i in range(N_COPY):
-        copies[i].wait_send()
+
+        @pl.when(near(*steps[i]))
+        def _():
+            copies[i].wait_send()
 
 
 def body(nf, nc, fluid_pop, heat_pop, solid_temp, material, cond, nbr, wall, snbr, sflu):
-    hbm = pl.BlockSpec(memory_space=pl.ANY)
-    smem = pl.BlockSpec(memory_space=pltpu.SMEM)
+    hbm = pl.BlockSpec(memory_space=pltpu.HBM)
 
     def vm(*shape):
         return pltpu.VMEM(shape, F32)
@@ -578,7 +632,7 @@
             jax.ShapeDtypeStruct(heat_pop.shape, F32),
             jax.ShapeDtypeStruct(solid_temp.shape, F32),
         ),
-        in_specs=[hbm] * 4 + [smem] * 5,
+        in_specs=[hbm] * 9,
         out_specs=(hbm, hbm, hbm),
         scratch_shapes=[
             vm(FB, 19, E, W),
@@ -602,13 +656,18 @@
             vm(2, 2, SB, W),
             vm(2, 2, E, H),
             vm(2, 2, E, H),
-            pltpu.SemaphoreType.DMA((8,)),
+            pltpu.SMEM(cond.shape, F32),
+            pltpu.SMEM(nbr.shape, jnp.int32),
+            pltpu.SMEM(wall.shape, jnp.int32),
+            pltpu.SMEM(snbr.shape, jnp.int32),
+            pltpu.SMEM(sflu.shape, jnp.int32),
+            pltpu.SemaphoreType.DMA((13,)),
             pltpu.SemaphoreType.DMA((7,)),
             pltpu.SemaphoreType.DMA((N_COPY,)),
             pltpu.SemaphoreType.DMA((N_COPY,)),
         ],
         compiler_params=pltpu.CompilerParams(
-            collective_id=0, has_side_effects=True, vmem_limit_bytes=32 * 1024 * 1024
+            collective_id=0, has_side_effects=True, vmem_limit_bytes=60 * 1024 * 1024
         ),
     )(fluid_pop, heat_pop, solid_temp, material, cond, nbr, wall, snbr, sflu)
 

time: 34.1 us -> 22.8 us (0.67)
  the two profiles are of different devices: /device:TPU:0 before, /device:TPU:24 now
where the time goes in v1:
time: 22.8 us; the launch traced here: 22.6 us
  Pallas kernels  18.1 us (79%)
  local copies, waits for them, and re-layouts  3.78 us (17%)
  between operations  0.66 us (3%)
    pallas_call x1, Pallas kernels, body(): pl.pallas_call(functools.partial(kernel, nf, nc), out_shape=(jax.ShapeDty...  18.1 us
    unnamed x7, local copies, waits for them, and re-layouts  3.78 us

profile of v1, /device:TPU:24, one launch (start us, length us, event | category | flops | bytes accessed | tf_op | source)
XLA Modules:
  0.0 22.6 jit_solution(10542581841621604756)
XLA Ops:
  0.6 18.1 %shard_map.112 = (f32[3,19,4096]{2,1,0:T(8,128)}, f32[3,7,4096]{2,1,0:T(8,128)}, f32[2,4096]{1,0:T(2,128)}) custom-call(f32[3,19,4096]{2,1,0:T(8,128)} %fluid_in.1, f32[3,7,4096]{2,1,0:T(8,128)} %heat_in.1, f32[2,4096]{1,0:T(2,128)} %temp_in.1, s32[2,4096]{1,0:T(2,128)} %mat_in.1, f32[8]{0:T(128)} %cond_in.1, s32[3,18]{1,0:T(4,128)} %nbr_in.1, ...), custom_call_target="tpu_custom_call" | custom-call | tf_op jit(solution)/shard_map/pallas_call | solution.py:628
  18.8 0.0 copy-start
  18.8 0.0 copy-start.1
  18.8 2.4 %copy.15 = f32[3,19,4096]{2,1,0:T(8,128)} copy(f32[3,19,4096]{2,1,0:T(8,128)} %get-tuple-element.6) | data formatting | bytes 1867776
  21.2 0.0 copy-done
  21.2 0.7 %copy.16 = f32[3,7,4096]{2,1,0:T(8,128)} copy(f32[3,7,4096]{2,1,0:T(8,128)S(1)} %copy-done) | data formatting | bytes 688128
  21.9 0.0 copy-done.1
  22.0 0.6 %copy.17 = f32[2,4096]{1,0:T(2,128)} copy(f32[2,4096]{1,0:T(2,128)S(1)} %copy-done.1) | data formatting | bytes 65536
Async XLA Ops:
  18.8 2.4 %copy-start = (f32[3,7,4096]{2,1,0:T(8,128)S(1)}, f32[3,7,4096]{2,1,0:T(8,128)}, u32[]{:S(2)}) copy-start(f32[3,7,4096]{2,1,0:T(8,128)} %get-tuple-element.7) | copy-start | bytes 1032196
  18.8 3.2 %copy-start.1 = (f32[2,4096]{1,0:T(2,128)S(1)}, f32[2,4096]{1,0:T(2,128)}, u32[]{:S(2)}) copy-start(f32[2,4096]{1,0:T(2,128)} %get-tuple-element.8) | copy-start | bytes 98308

commit v2 on v1

--- a/solution.py
+++ b/solution.py
@@ -45,6 +45,7 @@
 CORNER_SRC = [(0, 1, 1), (0, 2, 0), (1, 1, 0), (1, 2, 1)]
 CORNER_OF = {7: 0, 9: 1, 8: 2, 10: 3}
 N_COPY = 20
+LIMIT = 60 * 1024 * 1024
 
 
 def lroll(v, s):
@@ -130,17 +131,14 @@
     wall_in,
     snbr_in,
     sflu_in,
-    fluid_out,
-    heat_out,
-    solid_out,
+    GO,
+    QO,
+    TO,
     G,
     Q,
-    GO,
-    QO,
     T,
     M,
     KAP,
-    TO,
     XS,
     XR,
     YS,
@@ -160,7 +158,6 @@
     snbr,
     sflu,
     in_sem,
-    out_sem,
     send_sem,
     recv_sem,
 ):
@@ -585,33 +582,17 @@
                 GO[b, p, x : x + 1, :] = xf[r : r + 1]
             QO[b, 1 + side, x : x + 1, :] = xf[HEAT : HEAT + 1]
 
-    def put(src, dst, sem):
-        for x in range(E):
-            pltpu.make_async_copy(
-                src.at[..., x, :], dst.at[..., pl.ds(W * x, W)], sem
-            ).start()
-
-    def finish(b):
-        with jax.named_scope("stream"):
-            stream(b)
-        put(GO.at[b], fluid_out.at[b], out_sem.at[2 * b])
-        put(QO.at[b], heat_out.at[b], out_sem.at[2 * b + 1])
-
-    finish(0)
+    with jax.named_scope("stream"):
+        stream(0)
+        stream(1)
     sweep(0)
     share(1)
-    finish(1)
+    with jax.named_scope("stream"):
+        stream(2)
     sweep(1)
     for s in range(SB):
         TO[s] = sol[s]
-    put(TO, solid_out, out_sem.at[6])
-    finish(2)
-
-    with jax.named_scope("wait_stores"):
-        for b in range(FB):
-            all_of(GO.at[b], out_sem.at[2 * b]).wait()
-            all_of(QO.at[b], out_sem.at[2 * b + 1]).wait()
-        all_of(TO, out_sem.at[6]).wait()
+
     for i in range(N_COPY):
 
         @pl.when(near(*steps[i]))
@@ -619,29 +600,38 @@
             copies[i].wait_send()
 
 
+def store_kernel(fluid, heat, solid, fluid_out, heat_out, solid_out, sem):
+    pairs = [(fluid, fluid_out), (heat, heat_out), (solid, solid_out)]
+    for i, (src, dst) in enumerate(pairs):
+        for x in range(E):
+            pltpu.make_async_copy(
+                src.at[..., x, :], dst.at[..., pl.ds(W * x, W)], sem.at[i]
+            ).start()
+    for i, (src, dst) in enumerate(pairs):
+        pltpu.make_async_copy(src, src, sem.at[i]).wait()
+
+
 def body(nf, nc, fluid_pop, heat_pop, solid_temp, material, cond, nbr, wall, snbr, sflu):
     hbm = pl.BlockSpec(memory_space=pltpu.HBM)
 
     def vm(*shape):
         return pltpu.VMEM(shape, F32)
 
-    return pl.pallas_call(
+    vmem = pl.BlockSpec(memory_space=pltpu.VMEM)
+    fields = pl.pallas_call(
         functools.partial(kernel, nf, nc),
         out_shape=(
-            jax.ShapeDtypeStruct(fluid_pop.shape, F32),
-            jax.ShapeDtypeStruct(heat_pop.shape, F32),
-            jax.ShapeDtypeStruct(solid_temp.shape, F32),
+            vm(FB, 19, E, W),
+            vm(FB, 7, E, W),
+            vm(SB, E, W),
         ),
         in_specs=[hbm] * 9,
-        out_specs=(hbm, hbm, hbm),
+        out_specs=(vmem, vmem, vmem),
         scratch_shapes=[
-            vm(FB, 19, E, W),
-            vm(FB, 7, E, W),
             vm(FB, 19, E, W),
             vm(FB, 7, E, W),
             vm(SB, E, W),
             pltpu.VMEM((SB, E, W), jnp.int32),
-            vm(SB, E, W),
             vm(SB, E, W),
             vm(2, FB, 8, W),
             vm(2, FB, 8, W),
@@ -662,14 +652,25 @@
             pltpu.SMEM(snbr.shape, jnp.int32),
             pltpu.SMEM(sflu.shape, jnp.int32),
             pltpu.SemaphoreType.DMA((13,)),
-            pltpu.SemaphoreType.DMA((7,)),
             pltpu.SemaphoreType.DMA((N_COPY,)),
             pltpu.SemaphoreType.DMA((N_COPY,)),
         ],
         compiler_params=pltpu.CompilerParams(
-            collective_id=0, has_side_effects=True, vmem_limit_bytes=60 * 1024 * 1024
+            collective_id=0, has_side_effects=True, vmem_limit_bytes=LIMIT
         ),
     )(fluid_pop, heat_pop, solid_temp, material, cond, nbr, wall, snbr, sflu)
+    return pl.pallas_call(
+        store_kernel,
+        out_shape=(
+            jax.ShapeDtypeStruct(fluid_pop.shape, F32),
+            jax.ShapeDtypeStruct(heat_pop.shape, F32),
+            jax.ShapeDtypeStruct(solid_temp.shape, F32),
+        ),
+        in_specs=[pl.BlockSpec(memory_space=pl.ANY)] * 3,
+        out_specs=(hbm, hbm, hbm),
+        scratch_shapes=[pltpu.SemaphoreType.DMA((3,))],
+        compiler_params=pltpu.CompilerParams(vmem_limit_bytes=8 * 1024 * 1024),
+    )(*fields)
 
 
 def solution(mesh):

time: 22.8 us -> 18.8 us (0.82)
  local copies, waits for them, and re-layouts: 3.78 us -> 0 us
    unnamed x7 -> x0, local copies, waits for them, and re-layouts: 3.78 us -> none
    pallas_call x1 -> x2, Pallas kernels: 18.1 us -> 17.9 us  [the longest x1 16.8 us: body(): pl.pallas_call(functools.partial(kernel, nf, nc), out_shape=(vm(FB, 19, E...]
where the time goes in v2:
time: 18.8 us; the launch traced here: 18.6 us
  Pallas kernels  17.9 us (95%)
  between operations  0.64 us (3%)
    pallas_call x1, Pallas kernels, body(): pl.pallas_call(functools.partial(kernel, nf, nc), out_shape=(vm(FB, 19, E...  16.8 us
    pallas_call x1, Pallas kernels, body(): pl.pallas_call(store_kernel, out_shape=(jax.ShapeDtypeStruct(fluid_pop.sh...  1.09 us

profile of v2, /device:TPU:24, one launch (start us, length us, event | category | flops | bytes accessed | tf_op | source)
XLA Modules:
  0.0 18.6 jit_solution(7722365458503709127)
XLA Ops:
  0.6 16.8 %shard_map.112 = (f32[3,19,16,256]{3,2,1,0:T(8,128)S(1)}, f32[3,7,16,256]{3,2,1,0:T(8,128)S(1)}, f32[2,16,256]{2,1,0:T(8,128)S(1)}) custom-call(f32[3,19,4096]{2,1,0:T(8,128)} %fluid_in.1, f32[3,7,4096]{2,1,0:T(8,128)} %heat_in.1, f32[2,4096]{1,0:T(2,128)} %temp_in.1, s32[2,4096]{1,0:T(2,128)} %mat_in.1, f32[8]{0:T(128)} %cond_in.1, s32[3,18]{1,0:T(4,128)} %nbr_in.1, ...), custom_call_target="tpu_custom_call" | custom-call | tf_op jit(solution)/shard_map/pallas_call | solution.py:621
  17.5 1.1 %shard_map.113 = (f32[3,19,4096]{2,1,0:T(8,128)}, f32[3,7,4096]{2,1,0:T(8,128)}, f32[2,4096]{1,0:T(2,128)}) custom-call(f32[3,19,16,256]{3,2,1,0:T(8,128)S(1)} %get-tuple-element.6.fluid, f32[3,7,16,256]{3,2,1,0:T(8,128)S(1)} %get-tuple-element.7.heat, f32[2,16,256]{2,1,0:T(8,128)S(1)} %get-tuple-element.8.solid), custom_call_target="tpu_custom_call" | custom-call | tf_op jit(solution)/shard_map/pallas_call | solution.py:662

commit v3 on v2

--- a/solution.py
+++ b/solution.py
@@ -44,7 +44,12 @@
 PEERS = SIDES + CORNERS
 CORNER_SRC = [(0, 1, 1), (0, 2, 0), (1, 1, 0), (1, 2, 1)]
 CORNER_OF = {7: 0, 9: 1, 8: 2, 10: 3}
-N_COPY = 20
+EDGE_Z = 6
+CROSS = 7
+N_COPY = 16
+NZ = 5
+EX = 24
+EL = 384
 LIMIT = 60 * 1024 * 1024
 
 
@@ -143,15 +148,25 @@
     XR,
     YS,
     YR,
+    CS,
     CR,
-    XTS,
-    XTR,
-    YTS,
-    YTR,
-    DXS,
-    DXR,
-    DYS,
-    DYR,
+    XES,
+    XER,
+    YES,
+    YER,
+    CER,
+    TE,
+    KE,
+    WE,
+    LX,
+    LY,
+    LZ,
+    R,
+    D,
+    SX,
+    SY,
+    SZ,
+    U,
     cond,
     nbr,
     wall,
@@ -163,7 +178,6 @@
 ):
     fl = lax.axis_index("flow")
     cr = lax.axis_index("cross")
-
     inside = {-1: (fl > 0, cr > 0), 0: (True, True), 1: (fl < nf - 1, cr < nc - 1)}
 
     def near(df, dc):
@@ -235,17 +249,67 @@
 
     wide = (E, W)
     lw = lanes(wide)
-    rw = rows(wide)
     zw = jnp.bitwise_and(lw, E - 1)
     lh = lanes((E, H))
+    zh = jnp.bitwise_and(lh, E - 1)
     group = jnp.right_shift(lh, 4)
+    r8 = rows((8, W))
+    l8 = lanes((8, W))
+    z8 = jnp.bitwise_and(l8, E - 1)
+    q8 = rows((8, H))
+    g8 = jnp.right_shift(lanes((8, H)), 4)
 
     def base_of(df, dc):
         return (fl + df) * nc + (cr + dc)
 
+    def slot(idv, base, n):
+        return jnp.clip(idv - base * n, 0, n - 1)
+
+    def num(flag):
+        return jnp.where(flag, 1, 0)
+
+    def on(flag, like):
+        return jnp.full(like.shape, flag) > 0
+
+    for c in tables:
+        c.wait()
+
+    here = base_of(0, 0)
+    below0 = sflu[0, 5]
+    below1 = sflu[1, 5]
+    z0 = jnp.where(below0 >= 0, slot(below0, here, FB) + 1, 0)
+    z1 = jnp.where(below1 >= 0, slot(below1, here, FB) + 2, z0 + 1)
+    own_z = (z0, z1)
+    flu_z = [b + num(b >= z0) + num(b + 1 >= z1) for b in range(FB)]
+
+    def column(za, zb, exists):
+        res = []
+        for p in range(NZ):
+            solid = num(jnp.logical_or(za == p, zb == p)) * exists
+            res.append(
+                (
+                    solid,
+                    exists - solid,
+                    num(zb == p),
+                    jnp.clip(p - num(za < p) - num(zb < p), 0, FB - 1),
+                )
+            )
+        return res
+
+    own = column(z0, z1, num(fl >= 0))
+    beside = []
+    for k in range(4):
+        df, dc = C[k + 1][0], C[k + 1][1]
+        first = base_of(df, dc) * SB
+        za = zb = 0
+        pairs = [(wall[b, k], flu_z[b]) for b in range(FB)]
+        pairs += [(snbr[s, k], own_z[s]) for s in range(SB)]
+        for idv, z in pairs:
+            za = za + jnp.where(idv == first, z, 0)
+            zb = zb + jnp.where(idv == first + 1, z, 0)
+        beside.append(column(za, zb, num(near(df, dc))))
+
     with jax.named_scope("wait_solid"):
-        for c in tables:
-            c.wait()
         all_of(T, in_sem.at[0]).wait()
         all_of(M, in_sem.at[1]).wait()
     for s in range(SB):
@@ -254,32 +318,34 @@
         for i in range(1, 8):
             k = jnp.where(m == i, cond[i], k)
         KAP[s] = k
-
-    def pack_y(pieces, side):
-        acc = None
-        for g, v in enumerate(pieces):
-            if side == 0:
-                r = lroll(v[:, H:], E * g - (H - E))
-            else:
-                r = lroll(v[:, :H], E * g)
-            acc = r if acc is None else jnp.where(group == g, r, acc)
-        return acc
-
-    for side in range(2):
-        x = E - 1 if side == 0 else 0
-        for s in range(SB):
-            XTS[side, s, 0:1, :] = T[s, x : x + 1, :]
-            XTS[side, s, 1:2, :] = KAP[s, x : x + 1, :]
-        YTS[side] = pack_y([T[0], KAP[0], T[1], KAP[1]], side)
+        zf = jnp.full((8, W), own_z[s]).astype(F32)
+        t = T[s]
+        XES[0, s] = jnp.where(r8 > 4, t[8:], jnp.where(r8 == 4, zf, rroll(k[8:], 4)))
+        XES[1, s] = jnp.where(r8 < 3, t[:8], jnp.where(r8 == 3, zf, rroll(k[:8], 4)))
+        YES[0, s] = jnp.where(lh >= 64, t[:, H:], lroll(k[:, H:], 64))
+        YES[1, s] = jnp.where(lh < 64, t[:, :H], lroll(k[:, :H], 64))
 
     with jax.named_scope("entry_barrier"):
         pl.semaphore_wait(barrier, n_peers)
     for i, (df, dc) in enumerate(SIDES):
         side = i % 2
         if i < 2:
-            send(i, XTS.at[side], XTR.at[side], df, dc)
+            send(i, XES.at[side], XER.at[side], df, dc)
         else:
-            send(i, YTS.at[side], YTR.at[side], df, dc)
+            send(i, YES.at[side], YER.at[side], df, dc)
+    for i, (df, dc) in enumerate(CORNERS):
+        side, _, half = CORNER_SRC[i]
+        send(4 + i, XES.at[side, :, :, pl.ds(H * half, H)], CER.at[i], df, dc)
+
+    def pack_y(pieces, side):
+        acc = None
+        for g, v in enumerate(pieces):
+            r = lroll(v, E * g - (H - E)) if side == 0 else lroll(v, E * g)
+            acc = r if acc is None else jnp.where(group == g, r, acc)
+        return acc
+
+    def two(v, first, second, z):
+        return jnp.where((z == 0) | (z == E - 1), v, jnp.where(z < 8, first, second))
 
     for b in range(FB):
         with jax.named_scope("wait_pops"):
@@ -291,79 +357,194 @@
                     collide_tile(G, Q, b, pl.ds(8 * xh, 8), pl.ds(H * yh, H))
         for side in range(2):
             x = E - 1 if side == 0 else 0
+            inner = E - 2 if side == 0 else 1
+
+            def line(x_at, lo, n):
+                zz = jnp.bitwise_and(lanes((1, n)), E - 1)
+                up = Q[b, 6, x_at : x_at + 1, lo : lo + n]
+                return jnp.where(zz < 8, up, Q[b, 5, x_at : x_at + 1, lo : lo + n])
+
             for r in range(5):
                 XS[side, b, r : r + 1, :] = G[b, PX[side][r], x : x + 1, :]
             XS[side, b, HEAT : HEAT + 1, :] = Q[b, 1 + side, x : x + 1, :]
+            z1w = jnp.bitwise_and(lanes((1, W)), E - 1)
+            v = line(inner, 0, W)
+            XS[side, b, EDGE_Z : EDGE_Z + 1, :] = two(
+                line(x, 0, W), lroll(v, 1), lroll(v, -1), z1w
+            )
+            XS[side, b, CROSS : CROSS + 1, :H] = Q[b, 4, x : x + 1, :H]
+            XS[side, b, CROSS : CROSS + 1, H:] = Q[b, 3, x : x + 1, H:]
+
+            half = pl.ds(H, H) if side == 0 else pl.ds(0, H)
+            sgn = 1 if side == 0 else -1
+            hz = jnp.where(zh < 8, Q[b, 6, :, half], Q[b, 5, :, half])
+            hx = jnp.concatenate([Q[b, 2, 0:8, half], Q[b, 1, 8:16, half]], axis=0)
             YS[side, b] = pack_y(
-                [G[b, PY[side][r]] for r in range(5)] + [Q[b, 3 + side]], side
+                [G[b, PY[side][r], :, half] for r in range(5)]
+                + [
+                    Q[b, 3 + side, :, half],
+                    two(hz, lroll(hz, sgn * E + 1), lroll(hz, sgn * E - 1), zh),
+                    hx,
+                ],
+                side,
             )
+            for i in range(4):
+                cs, row, ch = CORNER_SRC[i]
+                if cs != side:
+                    continue
+                sg = -1 if ch else 1
+                hp = 3 if ch else 4
+                lo = H * ch
+                gg = jnp.right_shift(lanes((1, H)), 4)
+                at = (lambda d: 7 - d) if ch else (lambda d: d)
+                acc = Q[b, 1 + side, x : x + 1, lo : lo + H]
+                extra = [
+                    (2, line(x, lo, H)),
+                    (3, G[b, PX[side][row], x : x + 1, lo : lo + H]),
+                    (4, Q[b, hp, x : x + 1, lo : lo + H]),
+                    (5, Q[b, hp, inner : inner + 1, lo : lo + H]),
+                ]
+                for d, v in extra:
+                    acc = jnp.where(gg == at(d), lroll(v, sg * E * d), acc)
+                CS[i, b] = acc
 
     for i, (df, dc) in enumerate(SIDES):
         side = i % 2
         if i < 2:
-            send(4 + i, XS.at[side], XR.at[side], df, dc)
+            send(8 + i, XS.at[side], XR.at[side], df, dc)
         else:
-            send(4 + i, YS.at[side], YR.at[side], df, dc)
+            send(8 + i, YS.at[side], YR.at[side], df, dc)
     for i, (df, dc) in enumerate(CORNERS):
-        side, r, half = CORNER_SRC[i]
-        send(
-            8 + i,
-            XS.at[side, :, pl.ds(r, 1), pl.ds(H * half, H)],
-            CR.at[i],
-            df,
-            dc,
+        send(12 + i, CS.at[i], CR.at[i], df, dc)
+
+    def stream(b):
+        def main(ref, p):
+            cx, cy, cz = C[p]
+            s = E * cy + cz
+            out = lroll(rroll(ref[b, p], cx), s)
+            if cz:
+                back = ref[b, OPP[p]]
+                adj = (b - cz) % FB
+                if ref is Q:
+                    wid = wall[b, (6 if cz > 0 else 5) - 1]
+                    tw = lroll(T[slot(wid, here, SB)], -(E - 1) * cz)
+                    back = jnp.where(jnp.full(wide, wid) >= 0, 2.0 * tw - back, back)
+                if 0 <= b - cz < FB:
+                    other = lroll(rroll(ref[adj, p], cx), E * cy - (E - 1) * cz)
+                    zid = nbr[b, (6 if cz > 0 else 5) - 1]
+                    back = jnp.where(jnp.full(wide, zid) >= 0, other, back)
+                edge = zw == 0 if cz > 0 else zw == E - 1
+                out = jnp.where(edge, back, out)
+            return out
+
+        GO[b, 0] = G[b, 0]
+        QO[b, 0] = Q[b, 0]
+        for p in range(1, 19):
+            GO[b, p] = main(G, p)
+        for p in range(1, 7):
+            QO[b, p] = main(Q, p)
+
+    with jax.named_scope("stream"):
+        for b in range(FB):
+            stream(b)
+
+    ext = (EX, EL)
+    ze = jnp.bitwise_and(lanes(ext), E - 1)
+
+    def piece(flag, v):
+        return jnp.where(on(flag, v), v, 0.0)
+
+    for i in range(8):
+        received(i)
+
+    def corner_z(i):
+        side = CORNER_SRC[i][0]
+        r = 4 if side == 0 else 3
+        return [
+            jnp.broadcast_to(CER[i, s, r : r + 1, :], (8, H))
+            for s in range(SB)
+        ]
+
+    quad = [[2, 3], [1, 0]]
+    cz = [corner_z(i) for i in range(4)]
+    chas = [jnp.full((8, H), num(near(-df, -dc))) > 0 for df, dc in CORNERS]
+
+    def quadrants(fn):
+        up = jnp.where(g8 < 4, fn(quad[0][0]), fn(quad[0][1]))
+        down = jnp.where(g8 < 4, fn(quad[1][0]), fn(quad[1][1]))
+        return jnp.where(q8 < 4, up, down)
+
+    for p in range(NZ):
+        solid, wet, ss, _ = own[p]
+        TE[p, 0:E, 0:W] = piece(solid, T[ss])
+        KE[p, 0:E, 0:W] = piece(solid, KAP[ss])
+        WE[p, 0:E, 0:W] = jnp.full(wide, wet).astype(F32)
+        a = piece(beside[0][p][0], XER[1, beside[0][p][2]])
+        c = piece(beside[1][p][0], XER[0, beside[1][p][2]])
+        TE[p, E:EX, 0:W] = jnp.where(r8 < 4, a, c)
+        KE[p, E:EX, 0:W] = rroll(jnp.where(r8 < 4, c, a), 4)
+        WE[p, E:EX, 0:W] = jnp.where(
+            r8 < 4, jnp.full((8, W), beside[0][p][1]), jnp.full((8, W), beside[1][p][1])
+        ).astype(F32)
+        a = piece(beside[2][p][0], YER[1, beside[2][p][2]])
+        c = piece(beside[3][p][0], YER[0, beside[3][p][2]])
+        TE[p, 0:E, W:EL] = jnp.where(group < 4, a, c)
+        KE[p, 0:E, W:EL] = lroll(jnp.where(group < 4, c, a), 64)
+        WE[p, 0:E, W:EL] = jnp.where(
+            group < 4,
+            jnp.full((E, H), beside[2][p][1]),
+            jnp.full((E, H), beside[3][p][1]),
+        ).astype(F32)
+
+        def corner_solid(i):
+            v = jnp.where(cz[i][1] == p, CER[i, 1], 0.0)
+            v = jnp.where(cz[i][0] == p, CER[i, 0], v)
+            return jnp.where(chas[i], v, 0.0)
+
+        def corner_wet(i):
+            return jnp.where(chas[i] & (cz[i][0] != p) & (cz[i][1] != p), 1.0, 0.0)
+
+        TE[p, E:EX, W:EL] = quadrants(corner_solid)
+        KE[p, E:EX, W:EL] = quadrants(lambda i: rroll(corner_solid(i), 4))
+        WE[p, E:EX, W:EL] = quadrants(corner_wet)
+
+    def z_up(ref, p):
+        v = lroll(ref[p], -1)
+        over = lroll(ref[p + 1], E - 1) if p + 1 < NZ else 0.0
+        return jnp.where(ze == E - 1, over, v)
+
+    def z_down(v, before):
+        under = lroll(before, 1 - E) if before is not None else 0.0
+        return jnp.where(ze == 0, under, lroll(v, 1))
+
+    def both(v, p, ref):
+        below = ref[p - 1] if p else None
+        return (
+            rroll(v, 1) + rroll(v, -1),
+            lroll(v, E) + lroll(v, -E),
+            z_up(ref, p) + z_down(v, below),
         )
 
-    def slot(idv, base, n):
-        return jnp.clip(idv - base * n, 0, n - 1)
-
-    def unpack_group(v, g, lo):
-        return lroll(v, -E * g) if lo else lroll(v, (H - E) - E * g)
-
-    def widen(v, lo):
-        return jnp.concatenate([v, v], axis=1)
-
-    def pick(sel, a, b_):
-        return jnp.where(jnp.full(a.shape, sel) == 0, a, b_)
-
-    edges = [rw == E - 1, rw == 0, lw >= W - E, lw < E, zw == E - 1, zw == 0]
-
-    def shifted(v, k):
-        return [
-            lambda: rroll(v, -1),
-            lambda: rroll(v, 1),
-            lambda: lroll(v, -E),
-            lambda: lroll(v, E),
-            lambda: lroll(v, -1),
-            lambda: lroll(v, 1),
-        ][k]()
-
-    def step_base(k):
-        return base_of(C[k + 1][0], C[k + 1][1])
-
-    def z_ghost(v, k):
-        return lroll(v, E - 1) if k == 4 else lroll(v, 1 - E)
-
-    def solid_ghost(k, s, sl, q, field):
-        if k < 2:
-            return XTR[1 - k, sl, q : q + 1, :]
-        if k < 4:
-            v = YTR[1 - (k - 2)]
-            lo = k == 3
-            return widen(pick(sl, unpack_group(v, q, lo), unpack_group(v, 2 + q, lo)), lo)
-        return z_ghost(field[1 - s], k)
-
-    def heat_ghost(k, fsl):
-        if k < 2:
-            return XR[1 - k, fsl, HEAT : HEAT + 1, :]
-        if k < 4:
-            lo = k == 3
-            return widen(unpack_group(YR[1 - (k - 2), fsl], HEAT, lo), lo)
-        return z_ghost(Q[fsl, 6 if k == 4 else 5], k)
-
-    with jax.named_scope("wait_faces"):
-        for i in range(12):
-            received(i)
+    def link(k, kb):
+        return (2.0 * k * kb) / jnp.maximum(k + kb, 0.05)
+
+    def divergence(v, up, p, before):
+        fx = LX[p] * (rroll(v, -1) - v)
+        fy = LY[p] * (lroll(v, -E) - v)
+        fz = LZ[p] * (up - v)
+        div = (fx - rroll(fx, 1)) + (fy - lroll(fy, E)) + (fz - z_down(fz, before))
+        return div, fz
+
+    before = None
+    for p in range(NZ):
+        k = KE[p]
+        LX[p] = link(k, rroll(k, -1))
+        LY[p] = link(k, lroll(k, -E))
+        LZ[p] = link(k, z_up(KE, p))
+        t = TE[p]
+        div, before = divergence(t, z_up(TE, p), p, before)
+        wx, wy, wz = both(WE[p], p, WE)
+        R[p] = div - jnp.where(k > 0.0, (wx + wy + wz) * t, 0.0)
 
     kmax = cond[0]
     for i in range(1, 8):
@@ -373,8 +554,8 @@
     sigma = center / radius
 
     def grow(v):
-        v = jnp.concatenate([v, v], axis=0)
-        return jnp.concatenate([v, v], axis=1)
+        v = jnp.concatenate([v] * (EX // 8), axis=0)
+        return jnp.concatenate([v] * (EL // H), axis=1)
 
     inv_center = grow(1.0 / center)
     rho0 = 1.0 / sigma
@@ -385,87 +566,85 @@
         (grow(rho2 * rho1), grow(2.0 * rho2 / radius)),
     ]
 
-    sid = [[snbr[s, k] for k in range(6)] for s in range(SB)]
-    fid = [[sflu[s, k] for k in range(6)] for s in range(SB)]
-    ssl = [[slot(sid[s][k], step_base(k), SB) for k in range(6)] for s in range(SB)]
-    links = []
-    resid = []
-    upd = []
-    sol = []
+    with jax.named_scope("wait_faces"):
+        for i in range(8, 16):
+            received(i)
+
+    def corner_heat(i, p):
+        f = p - jnp.where(cz[i][0] < p, 1, 0) - jnp.where(cz[i][1] < p, 1, 0)
+        a, b, c = [jnp.broadcast_to(CR[i, j], (8, H)) for j in range(FB)]
+        v = jnp.where(f <= 0, a, jnp.where(f == 1, b, c))
+        wet = chas[i] & (cz[i][0] != p) & (cz[i][1] != p)
+        return jnp.where(wet, v, 0.0)
+
+    row_edge = (q8 == 0) | (q8 == 7)
+    for p in range(NZ):
+        _, wet, _, f = own[p]
+        SX[p, 0:8, 0:W] = piece(wet, Q[f, 2, 0:8])
+        SX[p, 8:E, 0:W] = piece(wet, Q[f, 1, 8:E])
+        SY[p, 0:E, 0:H] = piece(wet, Q[f, 4, :, 0:H])
+        SY[p, 0:E, H:W] = piece(wet, Q[f, 3, :, H:W])
+        SZ[p, 0:E, 0:W] = piece(wet, jnp.where(zw < 8, Q[f, 6], Q[f, 5]))
+
+        def side_row(r):
+            v = []
+            for k in range(2):
+                _, w, _, g = beside[k][p]
+                row = jnp.broadcast_to(XR[1 - k, g, r : r + 1, :], (8, W))
+                v.append(piece(w, row))
+            return jnp.where(r8 < 4, v[0], v[1])
+
+        SX[p, E:EX, 0:W] = side_row(HEAT)
+        SY[p, E:EX, 0:W] = side_row(CROSS)
+        v = side_row(EDGE_Z)
+        SZ[p, E:EX, 0:W] = jnp.where(
+            (r8 == 0) | (r8 == 7), v, jnp.where(z8 < 8, lroll(v, -1), lroll(v, 1))
+        )
+        a = piece(beside[2][p][1], YR[1, beside[2][p][3]])
+        c = piece(beside[3][p][1], YR[0, beside[3][p][3]])
+        SX[p, 0:E, W:EL] = jnp.where(group < 4, lroll(a, E), c)
+        SY[p, 0:E, W:EL] = jnp.where(group < 4, lroll(a, -5 * E), lroll(c, 2 * E))
+        low = jnp.where(zh < 8, lroll(a, -5 * E - 1), lroll(a, 1 - 5 * E))
+        low = jnp.where(group == 0, lroll(a, -6 * E), low)
+        high = jnp.where(zh < 8, lroll(c, -1), lroll(c, 1))
+        high = jnp.where(group == 7, lroll(c, E), high)
+        SZ[p, 0:E, W:EL] = jnp.where(group < 4, low, high)
+
+        def sgn(i):
+            return 1 if CORNER_SRC[i][2] else -1
+
+        ch = [corner_heat(i, p) for i in range(4)]
+        SX[p, E:EX, W:EL] = quadrants(lambda i: ch[i])
+        SY[p, E:EX, W:EL] = quadrants(
+            lambda i: jnp.where(row_edge, lroll(ch[i], 4 * E), lroll(ch[i], sgn(i) * 5 * E))
+        )
+        SZ[p, E:EX, W:EL] = quadrants(lambda i: lroll(ch[i], sgn(i) * 2 * E))
+
+    for p in range(NZ):
+        sx, sy = SX[p], SY[p]
+        heat = (rroll(sx, 1) + rroll(sx, -1)) + (lroll(sy, E) + lroll(sy, -E))
+        heat = heat + (z_up(SZ, p) + z_down(SZ[p], SZ[p - 1] if p else None))
+        acc = R[p] + jnp.where(KE[p] > 0.0, heat, 0.0)
+        R[p] = acc
+        d = acc * inv_center
+        D[p] = d
+        U[p] = TE[p, 0:E, 0:W] + d[0:E, 0:W]
+    for n in range(2):
+        before = None
+        for p in range(NZ):
+            v = D[p]
+            div, before = divergence(v, z_up(D, p), p, before)
+            r = R[p] - (v - div)
+            d = coef[n][0] * v + coef[n][1] * r
+            if n == 0:
+                R[p] = r
+                D[p] = d
+            U[p] = U[p] + d[0:E, 0:W]
     for s in range(SB):
-        t = T[s]
-        kap = KAP[s]
-        acc = jnp.zeros(wide, F32)
-        row = []
-        for k in range(6):
-            sl = ssl[s][k]
-            live = jnp.full(wide, sid[s][k]) >= 0
-            wet = jnp.full(wide, fid[s][k]) >= 0
-            kb = jnp.where(edges[k], solid_ghost(k, s, sl, 1, KAP), shifted(kap, k))
-            link = (2.0 * kap * kb) / (kap + kb)
-            link = jnp.where(edges[k] & ~live, 0.0, link)
-            row.append(link)
-            tb = jnp.where(edges[k], solid_ghost(k, s, sl, 0, T), shifted(t, k))
-            hb = heat_ghost(k, slot(fid[s][k], step_base(k), FB))
-            tb = jnp.where(edges[k] & ~live, t, tb)
-            wet_edge = edges[k] & wet
-            acc = acc + jnp.where(wet_edge, 1.0, link) * (jnp.where(wet_edge, hb, tb) - t)
-        links.append(row)
-        d = acc * inv_center
-        resid.append(acc)
-        upd.append(d)
-        sol.append(t + d)
-
-    def share(n):
-        for side in range(2):
-            x = E - 1 if side == 0 else 0
-            for s in range(SB):
-                DXS[n, side, s : s + 1, :] = upd[s][x : x + 1, :]
-            DYS[n, side] = pack_y(upd, side)
-        for i, (df, dc) in enumerate(SIDES):
-            side = i % 2
-            if i < 2:
-                send(12 + 4 * n + i, DXS.at[n, side], DXR.at[n, side], df, dc)
-            else:
-                send(12 + 4 * n + i, DYS.at[n, side], DYR.at[n, side], df, dc)
-
-    def update_ghost(n, k, s, sl):
-        if k < 2:
-            v = DXR[n, 1 - k]
-            return pick(sl, v[0:1], v[1:2])
-        if k < 4:
-            v = DYR[n, 1 - (k - 2)]
-            lo = k == 3
-            return widen(pick(sl, unpack_group(v, 0, lo), unpack_group(v, 1, lo)), lo)
-        return z_ghost(upd[1 - s], k)
-
-    def sweep(n):
-        with jax.named_scope("wait_updates"):
-            for i in range(4):
-                received(12 + 4 * n + i)
-        fresh = []
-        for s in range(SB):
-            d = upd[s]
-            acc = d
-            for k in range(6):
-                ghost = update_ghost(n, k, s, ssl[s][k])
-                ghost = jnp.where(jnp.full(ghost.shape, sid[s][k]) >= 0, ghost, 0.0)
-                db = jnp.where(edges[k], ghost, shifted(d, k))
-                acc = acc + links[s][k] * (d - db)
-            resid[s] = resid[s] - acc
-            nd = coef[n][0] * d + coef[n][1] * resid[s]
-            fresh.append(nd)
-            sol[s] = sol[s] + nd
-        for s in range(SB):
-            upd[s] = fresh[s]
-
-    share(0)
+        TO[s] = U[own_z[s]]
 
     def x_face(b, side):
         shape = (8, W)
-        r8 = rows(shape)
-        l8 = lanes(shape)
-        z8 = jnp.bitwise_and(l8, E - 1)
         df = -1 if side == 0 else 1
         dirn = 2 if side == 0 else 1
         bf = base_of(df, 0)
@@ -477,12 +656,10 @@
             _, cy, cz = C[p]
             if r == 0:
                 continue
-            src = OPP[p]
-            cid = nbr[b, src - 1]
+            cid = nbr[b, OPP[p] - 1]
             if cy:
                 corner = CR[CORNER_OF[p], slot(cid, base_of(df, -cy), FB)]
-                corner = jnp.broadcast_to(corner, (8, H))
-                corner = lroll(corner, E * cy)
+                corner = lroll(jnp.broadcast_to(corner, (8, H)), 4 * E)
                 corner = jnp.concatenate([corner, corner], axis=1)
                 edge = l8 < E if cy > 0 else l8 >= W - E
                 cand = jnp.where(edge, corner, lroll(a, E * cy))
@@ -494,14 +671,14 @@
             ids = jnp.where((r8 == r) & edge, jnp.full(shape, cid), ids)
         fall = XS[1 - side, b]
         wid = wall[b, dirn - 1]
-        tw = XTR[side, slot(wid, bf, SB), 0:1, :]
+        row = 7 if side == 0 else 0
+        tw = XER[side, slot(wid, bf, SB), row : row + 1, :]
         hot = (r8 == HEAT) & (jnp.full(shape, wid) >= 0)
         fall = jnp.where(hot, 2.0 * tw - fall, fall)
         return jnp.where(ids >= 0, val, fall)
 
     def y_face(b, side):
         shape = (E, H)
-        zh = jnp.bitwise_and(lh, E - 1)
         dc = -1 if side == 0 else 1
         dirn = 4 if side == 0 else 3
         bf = base_of(0, dc)
@@ -524,74 +701,29 @@
             ids = jnp.where((group == r) & edge, jnp.full(shape, cid), ids)
         fall = YS[1 - side, b]
         wid = wall[b, dirn - 1]
-        wsl = slot(wid, bf, SB)
-        tv = YTR[side]
-        tw = pick(wsl, lroll(tv, E * HEAT), lroll(tv, E * (HEAT - 2)))
+        tw = YER[side, slot(wid, bf, SB)]
+        tw = lroll(tw, -2 * E if side == 0 else HEAT * E)
         hot = (group == HEAT) & (jnp.full(shape, wid) >= 0)
         fall = jnp.where(hot, 2.0 * tw - fall, fall)
         return jnp.where(ids >= 0, val, fall)
 
-    def stream(b):
-        yf = [y_face(b, 0), y_face(b, 1)]
-
-        def main(ref, p, q):
-            cx, cy, cz = C[p]
-            s = E * cy + cz
-            out = lroll(rroll(ref[b, p], cx), s)
-            if cz:
-                back = ref[b, OPP[p]]
-                adj = (b - cz) % FB
-                if 0 <= b - cz < FB:
-                    other = lroll(rroll(ref[adj, p], cx), E * cy - (E - 1) * cz)
-                    zid = nbr[b, (6 if cz > 0 else 5) - 1]
-                else:
-                    other = None
-                if ref is Q:
-                    wid = wall[b, (6 if cz > 0 else 5) - 1]
-                    tw = lroll(T[slot(wid, base_of(0, 0), SB)], -(E - 1) * cz)
-                    back = jnp.where(jnp.full(wide, wid) >= 0, 2.0 * tw - back, back)
-                if other is not None:
-                    back = jnp.where(jnp.full(wide, zid) >= 0, other, back)
-                edge = zw == 0 if cz > 0 else zw == E - 1
-                out = jnp.where(edge, back, out)
-            if cy:
-                lo = cy > 0
-                v = unpack_group(yf[0 if lo else 1], q, lo)
-                if lo:
-                    out = jnp.concatenate(
-                        [jnp.where(lh < E, v, out[:, :H]), out[:, H:]], axis=1
-                    )
-                else:
-                    out = jnp.concatenate(
-                        [out[:, :H], jnp.where(lh >= H - E, v, out[:, H:])], axis=1
-                    )
-            return out
-
-        GO[b, 0] = G[b, 0]
-        QO[b, 0] = Q[b, 0]
-        for p in range(1, 19):
-            cy = C[p][1]
-            q = PY[0 if cy > 0 else 1].index(p) if cy else None
-            GO[b, p] = main(G, p, q)
-        for p in range(1, 7):
-            QO[b, p] = main(Q, p, HEAT)
+    for b in range(FB):
+        for side in range(2):
+            yf = y_face(b, side)
+            half = pl.ds(0, H) if side == 0 else pl.ds(H, H)
+            edge = lh < E if side == 0 else lh >= H - E
+            back = 0 if side == 0 else H - E
+            for q, p in enumerate(PY[side]):
+                v = lroll(yf, back - E * q)
+                GO[b, p, :, half] = jnp.where(edge, v, GO[b, p, :, half])
+            v = lroll(yf, back - E * HEAT)
+            QO[b, 3 + side, :, half] = jnp.where(edge, v, QO[b, 3 + side, :, half])
         for side in range(2):
             xf = x_face(b, side)
             x = 0 if side == 0 else E - 1
             for r, p in enumerate(PX[side]):
                 GO[b, p, x : x + 1, :] = xf[r : r + 1]
             QO[b, 1 + side, x : x + 1, :] = xf[HEAT : HEAT + 1]
-
-    with jax.named_scope("stream"):
-        stream(0)
-        stream(1)
-    sweep(0)
-    share(1)
-    with jax.named_scope("stream"):
-        stream(2)
-    sweep(1)
-    for s in range(SB):
-        TO[s] = sol[s]
 
     for i in range(N_COPY):
 
@@ -638,14 +770,16 @@
             vm(2, FB, E, H),
             vm(2, FB, E, H),
             vm(4, FB, 1, H),
-            vm(2, SB, 2, W),
-            vm(2, SB, 2, W),
-            vm(2, E, H),
-            vm(2, E, H),
-            vm(2, 2, SB, W),
-            vm(2, 2, SB, W),
-            vm(2, 2, E, H),
-            vm(2, 2, E, H),
+            vm(4, FB, 1, H),
+            vm(2, SB, 8, W),
+            vm(2, SB, 8, W),
+            vm(2, SB, E, H),
+            vm(2, SB, E, H),
+            vm(4, SB, 8, H),
+        ]
+        + [vm(NZ, EX, EL)] * 11
+        + [
+            vm(NZ, E, W),
             pltpu.SMEM(cond.shape, F32),
             pltpu.SMEM(nbr.shape, jnp.int32),
             pltpu.SMEM(wall.shape, jnp.int32),

time: 18.8 us -> 14 us (0.74)
  Pallas kernels: 17.9 us -> 13.2 us
    pallas_call x1, Pallas kernels: 16.8 us -> 12.1 us  [body(): pl.pallas_call(functools.partial(kernel, nf, nc), out_shape=(vm(FB, 19, E...]
where the time goes in v3:
time: 14 us; the launch traced here: 13.9 us
  Pallas kernels  13.2 us (94%)
  between operations  0.64 us (5%)
    pallas_call x1, Pallas kernels, body(): pl.pallas_call(functools.partial(kernel, nf, nc), out_shape=(vm(FB, 19, E...  12.1 us
    pallas_call x1, Pallas kernels, body(): pl.pallas_call(store_kernel, out_shape=(jax.ShapeDtypeStruct(fluid_pop.sh...  1.09 us

profile of v3, /device:TPU:24, one launch (start us, length us, event | category | flops | bytes accessed | tf_op | source)
XLA Modules:
  0.0 13.9 jit_solution(14230026176920650515)
XLA Ops:
  0.6 12.1 %shard_map.112 = (f32[3,19,16,256]{3,2,1,0:T(8,128)S(1)}, f32[3,7,16,256]{3,2,1,0:T(8,128)S(1)}, f32[2,16,256]{2,1,0:T(8,128)S(1)}) custom-call(f32[3,19,4096]{2,1,0:T(8,128)} %fluid_in.1, f32[3,7,4096]{2,1,0:T(8,128)} %heat_in.1, f32[2,4096]{1,0:T(2,128)} %temp_in.1, s32[2,4096]{1,0:T(2,128)} %mat_in.1, f32[8]{0:T(128)} %cond_in.1, s32[3,18]{1,0:T(4,128)} %nbr_in.1, ...), custom_call_target="tpu_custom_call" | custom-call | tf_op jit(solution)/shard_map/pallas_call | solution.py:753
  12.8 1.1 %shard_map.113 = (f32[3,19,4096]{2,1,0:T(8,128)}, f32[3,7,4096]{2,1,0:T(8,128)}, f32[2,4096]{1,0:T(2,128)}) custom-call(f32[3,19,16,256]{3,2,1,0:T(8,128)S(1)} %get-tuple-element.6.fluid, f32[3,7,16,256]{3,2,1,0:T(8,128)S(1)} %get-tuple-element.7.heat, f32[2,16,256]{2,1,0:T(8,128)S(1)} %get-tuple-element.8.solid), custom_call_target="tpu_custom_call" | custom-call | tf_op jit(solution)/shard_map/pallas_call | solution.py:796

commit v4 on v3

--- a/solution.py
+++ b/solution.py
@@ -48,6 +48,7 @@
 CROSS = 7
 N_COPY = 16
 NZ = 5
+NONE = -9
 EX = 24
 EL = 384
 LIMIT = 60 * 1024 * 1024
@@ -157,16 +158,14 @@
     CER,
     TE,
     KE,
-    WE,
+    WX,
+    WY,
+    WZ,
     LX,
     LY,
     LZ,
     R,
-    D,
-    SX,
-    SY,
-    SZ,
-    U,
+    CODE,
     cond,
     nbr,
     wall,
@@ -282,22 +281,11 @@
     own_z = (z0, z1)
     flu_z = [b + num(b >= z0) + num(b + 1 >= z1) for b in range(FB)]
 
-    def column(za, zb, exists):
-        res = []
-        for p in range(NZ):
-            solid = num(jnp.logical_or(za == p, zb == p)) * exists
-            res.append(
-                (
-                    solid,
-                    exists - solid,
-                    num(zb == p),
-                    jnp.clip(p - num(za < p) - num(zb < p), 0, FB - 1),
-                )
-            )
-        return res
-
-    own = column(z0, z1, num(fl >= 0))
-    beside = []
+    def fluid_slot(za, zb, z):
+        return jnp.clip(z - num(za < z) - num(zb < z), 0, FB - 1)
+
+    nbr_z = []
+    nbr_has = []
     for k in range(4):
         df, dc = C[k + 1][0], C[k + 1][1]
         first = base_of(df, dc) * SB
@@ -307,7 +295,9 @@
         for idv, z in pairs:
             za = za + jnp.where(idv == first, z, 0)
             zb = zb + jnp.where(idv == first + 1, z, 0)
-        beside.append(column(za, zb, num(near(df, dc))))
+        has = num(near(df, dc))
+        nbr_has.append(has)
+        nbr_z.append((jnp.where(has > 0, za, NONE), jnp.where(has > 0, zb, NONE)))
 
     with jax.named_scope("wait_solid"):
         all_of(T, in_sem.at[0]).wait()
@@ -466,85 +456,103 @@
         ]
 
     quad = [[2, 3], [1, 0]]
-    cz = [corner_z(i) for i in range(4)]
     chas = [jnp.full((8, H), num(near(-df, -dc))) > 0 for df, dc in CORNERS]
+    cz = [[jnp.where(chas[i], v, float(NONE)) for v in corner_z(i)] for i in range(4)]
 
     def quadrants(fn):
         up = jnp.where(g8 < 4, fn(quad[0][0]), fn(quad[0][1]))
         down = jnp.where(g8 < 4, fn(quad[1][0]), fn(quad[1][1]))
         return jnp.where(q8 < 4, up, down)
 
-    for p in range(NZ):
-        solid, wet, ss, _ = own[p]
-        TE[p, 0:E, 0:W] = piece(solid, T[ss])
-        KE[p, 0:E, 0:W] = piece(solid, KAP[ss])
-        WE[p, 0:E, 0:W] = jnp.full(wide, wet).astype(F32)
-        a = piece(beside[0][p][0], XER[1, beside[0][p][2]])
-        c = piece(beside[1][p][0], XER[0, beside[1][p][2]])
-        TE[p, E:EX, 0:W] = jnp.where(r8 < 4, a, c)
-        KE[p, E:EX, 0:W] = rroll(jnp.where(r8 < 4, c, a), 4)
-        WE[p, E:EX, 0:W] = jnp.where(
-            r8 < 4, jnp.full((8, W), beside[0][p][1]), jnp.full((8, W), beside[1][p][1])
-        ).astype(F32)
-        a = piece(beside[2][p][0], YER[1, beside[2][p][2]])
-        c = piece(beside[3][p][0], YER[0, beside[3][p][2]])
-        TE[p, 0:E, W:EL] = jnp.where(group < 4, a, c)
-        KE[p, 0:E, W:EL] = lroll(jnp.where(group < 4, c, a), 64)
-        WE[p, 0:E, W:EL] = jnp.where(
-            group < 4,
-            jnp.full((E, H), beside[2][p][1]),
-            jnp.full((E, H), beside[3][p][1]),
-        ).astype(F32)
+    def splat(shape, v):
+        return jnp.full(shape, v).astype(F32)
+
+    Z = []
+    for s in range(SB):
+        TE[s, 0:E, 0:W] = T[s]
+        KE[s, 0:E, 0:W] = KAP[s]
+        a = piece(nbr_has[0], XER[1, s])
+        c = piece(nbr_has[1], XER[0, s])
+        TE[s, E:EX, 0:W] = jnp.where(r8 < 4, a, c)
+        KE[s, E:EX, 0:W] = rroll(jnp.where(r8 < 4, c, a), 4)
+        zx = jnp.where(r8 < 4, splat((8, W), nbr_z[0][s]), splat((8, W), nbr_z[1][s]))
+        a = piece(nbr_has[2], YER[1, s])
+        c = piece(nbr_has[3], YER[0, s])
+        TE[s, 0:E, W:EL] = jnp.where(group < 4, a, c)
+        KE[s, 0:E, W:EL] = lroll(jnp.where(group < 4, c, a), 64)
+        zy = jnp.where(group < 4, splat((E, H), nbr_z[2][s]), splat((E, H), nbr_z[3][s]))
 
         def corner_solid(i):
-            v = jnp.where(cz[i][1] == p, CER[i, 1], 0.0)
-            v = jnp.where(cz[i][0] == p, CER[i, 0], v)
-            return jnp.where(chas[i], v, 0.0)
-
-        def corner_wet(i):
-            return jnp.where(chas[i] & (cz[i][0] != p) & (cz[i][1] != p), 1.0, 0.0)
-
-        TE[p, E:EX, W:EL] = quadrants(corner_solid)
-        KE[p, E:EX, W:EL] = quadrants(lambda i: rroll(corner_solid(i), 4))
-        WE[p, E:EX, W:EL] = quadrants(corner_wet)
-
-    def z_up(ref, p):
-        v = lroll(ref[p], -1)
-        over = lroll(ref[p + 1], E - 1) if p + 1 < NZ else 0.0
-        return jnp.where(ze == E - 1, over, v)
-
-    def z_down(v, before):
-        under = lroll(before, 1 - E) if before is not None else 0.0
-        return jnp.where(ze == 0, under, lroll(v, 1))
-
-    def both(v, p, ref):
-        below = ref[p - 1] if p else None
-        return (
-            rroll(v, 1) + rroll(v, -1),
-            lroll(v, E) + lroll(v, -E),
-            z_up(ref, p) + z_down(v, below),
-        )
+            return jnp.where(chas[i], CER[i, s], 0.0)
+
+        TE[s, E:EX, W:EL] = quadrants(corner_solid)
+        KE[s, E:EX, W:EL] = quadrants(lambda i: rroll(corner_solid(i), 4))
+        top = jnp.concatenate([splat(wide, own_z[s]), zy], axis=1)
+        low = jnp.concatenate([zx, quadrants(lambda i: cz[i][s])], axis=1)
+        Z.append(jnp.concatenate([top, low], axis=0))
 
     def link(k, kb):
         return (2.0 * k * kb) / jnp.maximum(k + kb, 0.05)
 
-    def divergence(v, up, p, before):
-        fx = LX[p] * (rroll(v, -1) - v)
-        fy = LY[p] * (lroll(v, -E) - v)
-        fz = LZ[p] * (up - v)
-        div = (fx - rroll(fx, 1)) + (fy - lroll(fy, E)) + (fz - z_down(fz, before))
-        return div, fz
-
-    before = None
-    for p in range(NZ):
-        k = KE[p]
-        LX[p] = link(k, rroll(k, -1))
-        LY[p] = link(k, lroll(k, -E))
-        LZ[p] = link(k, z_up(KE, p))
-        t = TE[p]
-        div, before = divergence(t, z_up(TE, p), p, before)
-        wx, wy, wz = both(WE[p], p, WE)
-        R[p] = div - jnp.where(k > 0.0, (wx + wy + wz) * t, 0.0)
+    def toward(k, v):
+        return rroll(v, -1 if k == 0 else 1) if k < 2 else lroll(v, -E if k == 2 else E)
+
+    wet = [[0.0, 0.0] for _ in range(SB)]
+    for k in range(4):
+        za, zb = toward(k, Z[0]), toward(k, Z[1])
+        for s in range(SB):
+            code = jnp.where(zb == Z[s], 1, jnp.where(za == Z[s], 0, 2))
+            CODE[k, s] = code
+            wet[s][k // 2] = jnp.where((code == 2) & (za >= 0.0), 1.0, wet[s][k // 2])
+    adj = Z[1] == Z[0] + 1.0
+    top, bottom = ze == E - 1, ze == 0
+    wet_z = [
+        (top & (~adj) & (Z[0] < NZ - 1.0) & (Z[0] >= 0.0)) | (bottom & (Z[0] > 0.0)),
+        (top & (Z[1] < NZ - 1.0) & (Z[1] >= 0.0)) | (bottom & (~adj) & (Z[1] >= 0.0)),
+    ]
+    for s in range(SB):
+        WX[s] = wet[s][0]
+        WY[s] = wet[s][1]
+        WZ[s] = jnp.where(wet_z[s], 1.0, 0.0)
+
+    def chosen(k, s, v):
+        code = CODE[k, s]
+        return jnp.where(code == 1, v[1], jnp.where(code == 0, v[0], 0.0))
+
+    def z_up(v):
+        return [jnp.where(top, lroll(v[1], E - 1), lroll(v[0], -1)), lroll(v[1], -1)]
+
+    def divergence(v):
+        div = []
+        for k, links in ((0, LX), (2, LY)):
+            over = [toward(k, x) for x in v]
+            f = [
+                links[s] * (jnp.where(CODE[k, s] == 1, over[1], over[0]) - v[s])
+                for s in range(SB)
+            ]
+            under = [toward(k + 1, x) for x in f]
+            part = [f[s] - chosen(k + 1, s, under) for s in range(SB)]
+            div = part if k == 0 else [a + b for a, b in zip(div, part)]
+        up = z_up(v)
+        f = [LZ[s] * (up[s] - v[s]) for s in range(SB)]
+        under = [
+            jnp.where(bottom, 0.0, lroll(f[0], 1)),
+            jnp.where(bottom, lroll(f[0], 1 - E), lroll(f[1], 1)),
+        ]
+        return [div[s] + (f[s] - under[s]) for s in range(SB)]
+
+    kk = [KE[s] for s in range(SB)]
+    for k, links in ((0, LX), (2, LY)):
+        over = [toward(k, x) for x in kk]
+        for s in range(SB):
+            links[s] = link(kk[s], chosen(k, s, over))
+    up = z_up(kk)
+    LZ[0] = link(kk[0], jnp.where(top & ~adj, 0.0, up[0]))
+    LZ[1] = link(kk[1], jnp.where(top, 0.0, up[1]))
+    tt = [TE[s] for s in range(SB)]
+    div = divergence(tt)
+    for s in range(SB):
+        R[s] = div[s] - (WX[s] + WY[s] + WZ[s]) * tt[s]
 
     kmax = cond[0]
     for i in range(1, 8):
@@ -570,78 +578,171 @@
         for i in range(8, 16):
             received(i)
 
-    def corner_heat(i, p):
-        f = p - jnp.where(cz[i][0] < p, 1, 0) - jnp.where(cz[i][1] < p, 1, 0)
+    def corner_heat(i, z):
+        f = z - jnp.where(cz[i][0] < z, 1.0, 0.0) - jnp.where(cz[i][1] < z, 1.0, 0.0)
         a, b, c = [jnp.broadcast_to(CR[i, j], (8, H)) for j in range(FB)]
-        v = jnp.where(f <= 0, a, jnp.where(f == 1, b, c))
-        wet = chas[i] & (cz[i][0] != p) & (cz[i][1] != p)
-        return jnp.where(wet, v, 0.0)
+        return jnp.where(f < 0.5, a, jnp.where(f < 1.5, b, c))
+
+    def of_three(za, zb, z, fn):
+        f = z - jnp.where(za < z, 1.0, 0.0) - jnp.where(zb < z, 1.0, 0.0)
+        return jnp.where(f < 0.5, fn(0), jnp.where(f < 1.5, fn(1), fn(2)))
 
     row_edge = (q8 == 0) | (q8 == 7)
-    for p in range(NZ):
-        _, wet, _, f = own[p]
-        SX[p, 0:8, 0:W] = piece(wet, Q[f, 2, 0:8])
-        SX[p, 8:E, 0:W] = piece(wet, Q[f, 1, 8:E])
-        SY[p, 0:E, 0:H] = piece(wet, Q[f, 4, :, 0:H])
-        SY[p, 0:E, H:W] = piece(wet, Q[f, 3, :, H:W])
-        SZ[p, 0:E, 0:W] = piece(wet, jnp.where(zw < 8, Q[f, 6], Q[f, 5]))
-
-        def side_row(r):
-            v = []
-            for k in range(2):
-                _, w, _, g = beside[k][p]
-                row = jnp.broadcast_to(XR[1 - k, g, r : r + 1, :], (8, W))
-                v.append(piece(w, row))
-            return jnp.where(r8 < 4, v[0], v[1])
-
-        SX[p, E:EX, 0:W] = side_row(HEAT)
-        SY[p, E:EX, 0:W] = side_row(CROSS)
-        v = side_row(EDGE_Z)
-        SZ[p, E:EX, 0:W] = jnp.where(
-            (r8 == 0) | (r8 == 7), v, jnp.where(z8 < 8, lroll(v, -1), lroll(v, 1))
+    wide_edge = (r8 == 0) | (r8 == 7)
+
+    def stack(v):
+        return jnp.concatenate([v, v], axis=0)
+
+    for s in range(SB):
+        oz = own_z[s]
+        nz = [nbr_z[k][s] for k in range(4)]
+        ozf = splat((8, H), oz)
+        nzf = [splat((8, H), z) for z in nz]
+        f_side = [fluid_slot(nbr_z[k][0], nbr_z[k][1], oz) for k in range(4)]
+        f_own = [fluid_slot(z0, z1, nz[k]) for k in range(4)]
+
+        own_lo = jnp.broadcast_to(XR[0, f_side[1], HEAT : HEAT + 1, :], (8, W))
+        own_hi = jnp.broadcast_to(XR[1, f_side[0], HEAT : HEAT + 1, :], (8, W))
+        x_tile = jnp.where(
+            r8 < 4,
+            jnp.broadcast_to(Q[f_own[0], 1, E - 1 : E, :], (8, W)),
+            jnp.broadcast_to(Q[f_own[1], 2, 0:1, :], (8, W)),
         )
-        a = piece(beside[2][p][1], YR[1, beside[2][p][3]])
-        c = piece(beside[3][p][1], YR[0, beside[3][p][3]])
-        SX[p, 0:E, W:EL] = jnp.where(group < 4, lroll(a, E), c)
-        SY[p, 0:E, W:EL] = jnp.where(group < 4, lroll(a, -5 * E), lroll(c, 2 * E))
-        low = jnp.where(zh < 8, lroll(a, -5 * E - 1), lroll(a, 1 - 5 * E))
-        low = jnp.where(group == 0, lroll(a, -6 * E), low)
-        high = jnp.where(zh < 8, lroll(c, -1), lroll(c, 1))
-        high = jnp.where(group == 7, lroll(c, E), high)
-        SZ[p, 0:E, W:EL] = jnp.where(group < 4, low, high)
-
-        def sgn(i):
-            return 1 if CORNER_SRC[i][2] else -1
-
-        ch = [corner_heat(i, p) for i in range(4)]
-        SX[p, E:EX, W:EL] = quadrants(lambda i: ch[i])
-        SY[p, E:EX, W:EL] = quadrants(
-            lambda i: jnp.where(row_edge, lroll(ch[i], 4 * E), lroll(ch[i], sgn(i) * 5 * E))
+        y_lo = jnp.where(g8 < 4, corner_heat(1, nzf[2]), corner_heat(0, nzf[3]))
+        y_hi = jnp.where(g8 < 4, corner_heat(2, nzf[2]), corner_heat(3, nzf[3]))
+
+        def from_y(i):
+            half = CORNER_SRC[i][2]
+            k = 3 if half else 2
+            row = 0 if i < 2 else E - 1
+            v = of_three(
+                nbr_z[k][0],
+                nbr_z[k][1],
+                cz[i][s],
+                lambda j: jnp.broadcast_to(YR[1 - half, j, row : row + 1, :], (8, H))
+                if not half
+                else jnp.broadcast_to(YR[0, j, row : row + 1, :], (8, H)),
+            )
+            return v if half else lroll(v, E)
+
+        heat = jnp.concatenate(
+            [
+                jnp.concatenate([own_lo, y_lo], axis=1),
+                jnp.concatenate([own_hi, y_hi], axis=1),
+                jnp.concatenate([x_tile, quadrants(from_y)], axis=1),
+            ],
+            axis=0,
         )
-        SZ[p, E:EX, W:EL] = quadrants(lambda i: lroll(ch[i], sgn(i) * 2 * E))
-
-    for p in range(NZ):
-        sx, sy = SX[p], SY[p]
-        heat = (rroll(sx, 1) + rroll(sx, -1)) + (lroll(sy, E) + lroll(sy, -E))
-        heat = heat + (z_up(SZ, p) + z_down(SZ[p], SZ[p - 1] if p else None))
-        acc = R[p] + jnp.where(KE[p] > 0.0, heat, 0.0)
-        R[p] = acc
-        d = acc * inv_center
-        D[p] = d
-        U[p] = TE[p, 0:E, 0:W] + d[0:E, 0:W]
+        acc = R[s] + jnp.where(WX[s] > 0.5, heat, 0.0)
+
+        left = lroll(YR[0, f_side[3]], -5 * E)
+        right = lroll(YR[1, f_side[2]], 2 * E)
+
+        def from_corner(i, z):
+            v = corner_heat(i, z)
+            if CORNER_SRC[i][2]:
+                return jnp.where(row_edge, lroll(v, -3 * E), lroll(v, -2 * E))
+            return jnp.where(row_edge, lroll(v, 3 * E), lroll(v, 2 * E))
+
+        x_left = jnp.where(q8 < 4, from_corner(3, nzf[0]), from_corner(0, nzf[1]))
+        x_right = jnp.where(q8 < 4, from_corner(2, nzf[0]), from_corner(1, nzf[1]))
+        y_tile = jnp.where(
+            group < 4,
+            lroll(Q[f_own[2], 3, :, H:W], E),
+            lroll(Q[f_own[3], 4, :, 0:H], -E),
+        )
+
+        def from_x(i):
+            half = CORNER_SRC[i][2]
+            k = 1 if i < 2 else 0
+            lo = 0 if half else H
+            v = of_three(
+                nbr_z[k][0],
+                nbr_z[k][1],
+                cz[i][s],
+                lambda j: jnp.broadcast_to(
+                    XR[1 - k, j, CROSS : CROSS + 1, lo : lo + H], (8, H)
+                ),
+            )
+            return lroll(v, -E if half else E)
+
+        heat = jnp.concatenate(
+            [
+                jnp.concatenate([left, right, y_tile], axis=1),
+                jnp.concatenate([x_left, x_right, quadrants(from_x)], axis=1),
+            ],
+            axis=0,
+        )
+        acc = acc + jnp.where(WY[s] > 0.5, heat, 0.0)
+
+        def updown(k):
+            za, zb = nbr_z[k]
+            return fluid_slot(za, zb, nz[k] + 1), fluid_slot(za, zb, nz[k] - 1)
+
+        tile = jnp.where(
+            zw < 8,
+            lroll(Q[fluid_slot(z0, z1, oz - 1), 5], 1 - E),
+            lroll(Q[fluid_slot(z0, z1, oz + 1), 6], E - 1),
+        )
+        a, c = [], []
+        for k in range(2):
+            u, d = updown(k)
+            a.append(jnp.broadcast_to(XR[1 - k, u, EDGE_Z : EDGE_Z + 1, :], (8, W)))
+            c.append(jnp.broadcast_to(XR[1 - k, d, EDGE_Z : EDGE_Z + 1, :], (8, W)))
+        a = jnp.where(r8 < 4, a[0], a[1])
+        c = jnp.where(r8 < 4, c[0], c[1])
+        x_tile = jnp.where(
+            z8 < 8,
+            jnp.where(wide_edge, lroll(c, 1 - E), lroll(c, 2 - E)),
+            jnp.where(wide_edge, lroll(a, E - 1), lroll(a, E - 2)),
+        )
+        u, d = updown(2)
+        a, c = YR[1, u], YR[1, d]
+        y_up = jnp.where(
+            zh < 8,
+            jnp.where(group == 0, lroll(c, -7 * E + 1), lroll(c, -6 * E + 2)),
+            jnp.where(group == 0, lroll(a, -5 * E - 1), lroll(a, -4 * E - 2)),
+        )
+        u, d = updown(3)
+        a, c = YR[0, u], YR[0, d]
+        y_down = jnp.where(
+            zh < 8,
+            jnp.where(group == 7, lroll(c, 1), lroll(c, 2 - E)),
+            jnp.where(group == 7, lroll(a, 2 * E - 1), lroll(a, E - 2)),
+        )
+
+        def from_z(i):
+            shift = 2 * E if CORNER_SRC[i][2] else -2 * E
+            a = lroll(corner_heat(i, cz[i][s] + 1.0), shift + E - 1)
+            c = lroll(corner_heat(i, cz[i][s] - 1.0), shift + 1 - E)
+            return jnp.where(z8[:, :H] < 8, c, a)
+
+        heat = jnp.concatenate(
+            [
+                jnp.concatenate([tile, jnp.where(group < 4, y_up, y_down)], axis=1),
+                jnp.concatenate([x_tile, quadrants(from_z)], axis=1),
+            ],
+            axis=0,
+        )
+        R[s] = acc + jnp.where(WZ[s] > 0.5, heat, 0.0)
+
+    upd = []
+    sol = []
+    for s in range(SB):
+        d = R[s] * inv_center
+        upd.append(d)
+        sol.append(T[s] + d[0:E, 0:W])
     for n in range(2):
-        before = None
-        for p in range(NZ):
-            v = D[p]
-            div, before = divergence(v, z_up(D, p), p, before)
-            r = R[p] - (v - div)
-            d = coef[n][0] * v + coef[n][1] * r
+        div = divergence(upd)
+        for s in range(SB):
+            r = R[s] - (upd[s] - div[s])
+            d = coef[n][0] * upd[s] + coef[n][1] * r
             if n == 0:
-                R[p] = r
-                D[p] = d
-            U[p] = U[p] + d[0:E, 0:W]
+                R[s] = r
+            upd[s] = d
+            sol[s] = sol[s] + d[0:E, 0:W]
     for s in range(SB):
-        TO[s] = U[own_z[s]]
+        TO[s] = sol[s]
 
     def x_face(b, side):
         shape = (8, W)
@@ -777,9 +878,9 @@
             vm(2, SB, E, H),
             vm(4, SB, 8, H),
         ]
-        + [vm(NZ, EX, EL)] * 11
+        + [vm(SB, EX, EL)] * 9
         + [
-            vm(NZ, E, W),
+            pltpu.VMEM((4, SB, EX, EL), jnp.int32),
             pltpu.SMEM(cond.shape, F32),
             pltpu.SMEM(nbr.shape, jnp.int32),
             pltpu.SMEM(wall.shape, jnp.int32),

time: 14 us -> 12.5 us (0.89)
  Pallas kernels: 13.2 us -> 11.7 us
    pallas_call x1, Pallas kernels: 12.1 us -> 10.6 us  [body(): pl.pallas_call(functools.partial(kernel, nf, nc), out_shape=(vm(FB, 19, E...]
where the time goes in v4:
time: 12.5 us; the launch traced here: 12.3 us
  Pallas kernels  11.7 us (94%)
  between operations  0.64 us (5%)
    pallas_call x1, Pallas kernels, body(): pl.pallas_call(functools.partial(kernel, nf, nc), out_shape=(vm(FB, 19, E...  10.6 us
    pallas_call x1, Pallas kernels, body(): pl.pallas_call(store_kernel, out_shape=(jax.ShapeDtypeStruct(fluid_pop.sh...  1.09 us

profile of v4, /device:TPU:24, one launch (start us, length us, event | category | flops | bytes accessed | tf_op | source)
XLA Modules:
  0.0 12.3 jit_solution(18238929819714676155)
XLA Ops:
  0.6 10.6 %shard_map.112 = (f32[3,19,16,256]{3,2,1,0:T(8,128)S(1)}, f32[3,7,16,256]{3,2,1,0:T(8,128)S(1)}, f32[2,16,256]{2,1,0:T(8,128)S(1)}) custom-call(f32[3,19,4096]{2,1,0:T(8,128)} %fluid_in.1, f32[3,7,4096]{2,1,0:T(8,128)} %heat_in.1, f32[2,4096]{1,0:T(2,128)} %temp_in.1, s32[2,4096]{1,0:T(2,128)} %mat_in.1, f32[8]{0:T(128)} %cond_in.1, s32[3,18]{1,0:T(4,128)} %nbr_in.1, ...), custom_call_target="tpu_custom_call" | custom-call | tf_op jit(solution)/shard_map/pallas_call | solution.py:854
  11.2 1.1 %shard_map.113 = (f32[3,19,4096]{2,1,0:T(8,128)}, f32[3,7,4096]{2,1,0:T(8,128)}, f32[2,4096]{1,0:T(2,128)}) custom-call(f32[3,19,16,256]{3,2,1,0:T(8,128)S(1)} %get-tuple-element.6.fluid, f32[3,7,16,256]{3,2,1,0:T(8,128)S(1)} %get-tuple-element.7.heat, f32[2,16,256]{2,1,0:T(8,128)S(1)} %get-tuple-element.8.solid), custom_call_target="tpu_custom_call" | custom-call | tf_op jit(solution)/shard_map/pallas_call | solution.py:897

commit v5 on v4

--- a/solution.py
+++ b/solution.py
@@ -41,12 +41,12 @@
 HEAT = 5
 SIDES = [(1, 0), (-1, 0), (0, 1), (0, -1)]
 CORNERS = [(1, 1), (1, -1), (-1, -1), (-1, 1)]
-PEERS = SIDES + CORNERS
+PEERS = CORNERS + SIDES
 CORNER_SRC = [(0, 1, 1), (0, 2, 0), (1, 1, 0), (1, 2, 1)]
 CORNER_OF = {7: 0, 9: 1, 8: 2, 10: 3}
 EDGE_Z = 6
 CROSS = 7
-N_COPY = 16
+N_COPY = 8
 NZ = 5
 NONE = -9
 EX = 24
@@ -145,17 +145,14 @@
     T,
     M,
     KAP,
+    FX,
+    FY,
     XS,
     XR,
     YS,
     YR,
     CS,
     CR,
-    XES,
-    XER,
-    YES,
-    YER,
-    CER,
     TE,
     KE,
     WX,
@@ -208,20 +205,19 @@
         return pltpu.make_async_copy(ref, ref, sem)
 
     tables = [
-        (cond_in, cond, 8),
-        (nbr_in, nbr, 9),
-        (wall_in, wall, 10),
-        (snbr_in, snbr, 11),
-        (sflu_in, sflu, 12),
+        (cond_in, cond, 4),
+        (nbr_in, nbr, 5),
+        (wall_in, wall, 6),
+        (snbr_in, snbr, 7),
+        (sflu_in, sflu, 8),
     ]
     tables = [pltpu.make_async_copy(a, b, in_sem.at[i]) for a, b, i in tables]
     for c in tables:
         c.start()
     load(temp_in, T, in_sem.at[0])
     load(mat_in, M, in_sem.at[1])
-    for b in range(FB):
-        load(fluid_in.at[b], G.at[b], in_sem.at[2 + 2 * b])
-        load(heat_in.at[b], Q.at[b], in_sem.at[3 + 2 * b])
+    load(fluid_in, G, in_sem.at[2])
+    load(heat_in, Q, in_sem.at[3])
 
     copies = {}
     steps = {}
@@ -310,22 +306,10 @@
         KAP[s] = k
         zf = jnp.full((8, W), own_z[s]).astype(F32)
         t = T[s]
-        XES[0, s] = jnp.where(r8 > 4, t[8:], jnp.where(r8 == 4, zf, rroll(k[8:], 4)))
-        XES[1, s] = jnp.where(r8 < 3, t[:8], jnp.where(r8 == 3, zf, rroll(k[:8], 4)))
-        YES[0, s] = jnp.where(lh >= 64, t[:, H:], lroll(k[:, H:], 64))
-        YES[1, s] = jnp.where(lh < 64, t[:, :H], lroll(k[:, :H], 64))
-
-    with jax.named_scope("entry_barrier"):
-        pl.semaphore_wait(barrier, n_peers)
-    for i, (df, dc) in enumerate(SIDES):
-        side = i % 2
-        if i < 2:
-            send(i, XES.at[side], XER.at[side], df, dc)
-        else:
-            send(i, YES.at[side], YER.at[side], df, dc)
-    for i, (df, dc) in enumerate(CORNERS):
-        side, _, half = CORNER_SRC[i]
-        send(4 + i, XES.at[side, :, :, pl.ds(H * half, H)], CER.at[i], df, dc)
+        XS[0, FB + s] = jnp.where(r8 > 4, t[8:], jnp.where(r8 == 4, zf, rroll(k[8:], 4)))
+        XS[1, FB + s] = jnp.where(r8 < 3, t[:8], jnp.where(r8 == 3, zf, rroll(k[:8], 4)))
+        YS[0, FB + s] = jnp.where(lh >= 64, t[:, H:], lroll(k[:, H:], 64))
+        YS[1, FB + s] = jnp.where(lh < 64, t[:, :H], lroll(k[:, :H], 64))
 
     def pack_y(pieces, side):
         acc = None
@@ -334,13 +318,20 @@
             acc = r if acc is None else jnp.where(group == g, r, acc)
         return acc
 
+    def ahead(v, p, z):
+        _, cy, cz = C[p]
+        if cz:
+            edge = z == 0 if cz > 0 else z == E - 1
+            return jnp.where(edge, lroll(v, -(E - 1) * cz), lroll(v, cz))
+        return lroll(v, E * cy)
+
     def two(v, first, second, z):
         return jnp.where((z == 0) | (z == E - 1), v, jnp.where(z < 8, first, second))
 
+    with jax.named_scope("wait_pops"):
+        all_of(G, in_sem.at[2]).wait()
+        all_of(Q, in_sem.at[3]).wait()
     for b in range(FB):
-        with jax.named_scope("wait_pops"):
-            all_of(G.at[b], in_sem.at[2 + 2 * b]).wait()
-            all_of(Q.at[b], in_sem.at[3 + 2 * b]).wait()
         with jax.named_scope("collide"):
             for xh in range(2):
                 for yh in range(2):
@@ -355,21 +346,28 @@
                 return jnp.where(zz < 8, up, Q[b, 5, x_at : x_at + 1, lo : lo + n])
 
             for r in range(5):
-                XS[side, b, r : r + 1, :] = G[b, PX[side][r], x : x + 1, :]
-            XS[side, b, HEAT : HEAT + 1, :] = Q[b, 1 + side, x : x + 1, :]
+                FX[side, b, r : r + 1, :] = G[b, PX[side][r], x : x + 1, :]
+            FX[side, b, HEAT : HEAT + 1, :] = Q[b, 1 + side, x : x + 1, :]
             z1w = jnp.bitwise_and(lanes((1, W)), E - 1)
             v = line(inner, 0, W)
-            XS[side, b, EDGE_Z : EDGE_Z + 1, :] = two(
+            FX[side, b, EDGE_Z : EDGE_Z + 1, :] = two(
                 line(x, 0, W), lroll(v, 1), lroll(v, -1), z1w
             )
-            XS[side, b, CROSS : CROSS + 1, :H] = Q[b, 4, x : x + 1, :H]
-            XS[side, b, CROSS : CROSS + 1, H:] = Q[b, 3, x : x + 1, H:]
+            FX[side, b, CROSS : CROSS + 1, :H] = Q[b, 4, x : x + 1, :H]
+            FX[side, b, CROSS : CROSS + 1, H:] = Q[b, 3, x : x + 1, H:]
+
+            raw = FX[side, b]
+            out = raw
+            for r, p in enumerate(PX[side]):
+                if r:
+                    out = jnp.where(r8 == r, ahead(raw, p, z8), out)
+            XS[side, b] = out
 
             half = pl.ds(H, H) if side == 0 else pl.ds(0, H)
             sgn = 1 if side == 0 else -1
             hz = jnp.where(zh < 8, Q[b, 6, :, half], Q[b, 5, :, half])
             hx = jnp.concatenate([Q[b, 2, 0:8, half], Q[b, 1, 8:16, half]], axis=0)
-            YS[side, b] = pack_y(
+            raw = pack_y(
                 [G[b, PY[side][r], :, half] for r in range(5)]
                 + [
                     Q[b, 3 + side, :, half],
@@ -378,6 +376,14 @@
                 ],
                 side,
             )
+            FY[side, b] = raw
+            out = raw
+            for q, p in enumerate(PY[side]):
+                cx = C[p][0]
+                if q:
+                    v = rroll(raw, cx) if cx else ahead(raw, p, zh)
+                    out = jnp.where(group == q, v, out)
+            YS[side, b] = out
             for i in range(4):
                 cs, row, ch = CORNER_SRC[i]
                 if cs != side:
@@ -390,22 +396,29 @@
                 acc = Q[b, 1 + side, x : x + 1, lo : lo + H]
                 extra = [
                     (2, line(x, lo, H)),
-                    (3, G[b, PX[side][row], x : x + 1, lo : lo + H]),
+                    (7, G[b, PX[side][row], x : x + 1, lo : lo + H]),
                     (4, Q[b, hp, x : x + 1, lo : lo + H]),
                     (5, Q[b, hp, inner : inner + 1, lo : lo + H]),
                 ]
                 for d, v in extra:
                     acc = jnp.where(gg == at(d), lroll(v, sg * E * d), acc)
-                CS[i, b] = acc
-
+                CS[i, 0, b : b + 1, :] = acc
+
+    for i in range(4):
+        side, _, ch = CORNER_SRC[i]
+        for s in range(SB):
+            CS[i, 1 + s] = XS[side, FB + s, :, H * ch : H * ch + H]
+
+    with jax.named_scope("entry_barrier"):
+        pl.semaphore_wait(barrier, n_peers)
+    for i, (df, dc) in enumerate(CORNERS):
+        send(4 + i, CS.at[i], CR.at[i], df, dc)
     for i, (df, dc) in enumerate(SIDES):
         side = i % 2
         if i < 2:
-            send(8 + i, XS.at[side], XR.at[side], df, dc)
+            send(i, XS.at[side], XR.at[side], df, dc)
         else:
-            send(8 + i, YS.at[side], YR.at[side], df, dc)
-    for i, (df, dc) in enumerate(CORNERS):
-        send(12 + i, CS.at[i], CR.at[i], df, dc)
+            send(i, YS.at[side], YR.at[side], df, dc)
 
     def stream(b):
         def main(ref, p):
@@ -444,14 +457,15 @@
     def piece(flag, v):
         return jnp.where(on(flag, v), v, 0.0)
 
-    for i in range(8):
-        received(i)
+    with jax.named_scope("wait_faces"):
+        for i in range(8):
+            received(i)
 
     def corner_z(i):
         side = CORNER_SRC[i][0]
         r = 4 if side == 0 else 3
         return [
-            jnp.broadcast_to(CER[i, s, r : r + 1, :], (8, H))
+            jnp.broadcast_to(CR[i, 1 + s, r : r + 1, :], (8, H))
             for s in range(SB)
         ]
 
@@ -471,19 +485,19 @@
     for s in range(SB):
         TE[s, 0:E, 0:W] = T[s]
         KE[s, 0:E, 0:W] = KAP[s]
-        a = piece(nbr_has[0], XER[1, s])
-        c = piece(nbr_has[1], XER[0, s])
+        a = piece(nbr_has[0], XR[1, FB + s])
+        c = piece(nbr_has[1], XR[0, FB + s])
         TE[s, E:EX, 0:W] = jnp.where(r8 < 4, a, c)
         KE[s, E:EX, 0:W] = rroll(jnp.where(r8 < 4, c, a), 4)
         zx = jnp.where(r8 < 4, splat((8, W), nbr_z[0][s]), splat((8, W), nbr_z[1][s]))
-        a = piece(nbr_has[2], YER[1, s])
-        c = piece(nbr_has[3], YER[0, s])
+        a = piece(nbr_has[2], YR[1, FB + s])
+        c = piece(nbr_has[3], YR[0, FB + s])
         TE[s, 0:E, W:EL] = jnp.where(group < 4, a, c)
         KE[s, 0:E, W:EL] = lroll(jnp.where(group < 4, c, a), 64)
         zy = jnp.where(group < 4, splat((E, H), nbr_z[2][s]), splat((E, H), nbr_z[3][s]))
 
         def corner_solid(i):
-            return jnp.where(chas[i], CER[i, s], 0.0)
+            return jnp.where(chas[i], CR[i, 1 + s], 0.0)
 
         TE[s, E:EX, W:EL] = quadrants(corner_solid)
         KE[s, E:EX, W:EL] = quadrants(lambda i: rroll(corner_solid(i), 4))
@@ -574,13 +588,13 @@
         (grow(rho2 * rho1), grow(2.0 * rho2 / radius)),
     ]
 
-    with jax.named_scope("wait_faces"):
-        for i in range(8, 16):
-            received(i)
+
+    def corner_rows(i):
+        return [jnp.broadcast_to(CR[i, 0, j : j + 1, :], (8, H)) for j in range(FB)]
 
     def corner_heat(i, z):
         f = z - jnp.where(cz[i][0] < z, 1.0, 0.0) - jnp.where(cz[i][1] < z, 1.0, 0.0)
-        a, b, c = [jnp.broadcast_to(CR[i, j], (8, H)) for j in range(FB)]
+        a, b, c = corner_rows(i)
         return jnp.where(f < 0.5, a, jnp.where(f < 1.5, b, c))
 
     def of_three(za, zb, z, fn):
@@ -732,17 +746,47 @@
         d = R[s] * inv_center
         upd.append(d)
         sol.append(T[s] + d[0:E, 0:W])
-    for n in range(2):
-        div = divergence(upd)
-        for s in range(SB):
-            r = R[s] - (upd[s] - div[s])
-            d = coef[n][0] * upd[s] + coef[n][1] * r
-            if n == 0:
-                R[s] = r
-            upd[s] = d
-            sol[s] = sol[s] + d[0:E, 0:W]
+    div = divergence(upd)
     for s in range(SB):
-        TO[s] = sol[s]
+        r = R[s] - (upd[s] - div[s])
+        R[s] = r
+        upd[s] = coef[0][0] * upd[s] + coef[0][1] * r
+        sol[s] = sol[s] + upd[s][0:E, 0:W]
+
+    v = [x[:, 0:W] for x in upd]
+    over = [rroll(x, -1) for x in v]
+    f = [
+        LX[s, :, 0:W] * (jnp.where(CODE[0, s, :, 0:W] == 1, over[1], over[0]) - v[s])
+        for s in range(SB)
+    ]
+    under = [rroll(x, 1)[0:E] for x in f]
+    code = [CODE[1, s, 0:E, 0:W] for s in range(SB)]
+    div = []
+    for s in range(SB):
+        u = jnp.where(code[s] == 1, under[1], jnp.where(code[s] == 0, under[0], 0.0))
+        div.append(f[s][0:E] - u)
+    v = [x[0:E] for x in upd]
+    over = [lroll(x, -E) for x in v]
+    f = [
+        LY[s, 0:E] * (jnp.where(CODE[2, s, 0:E] == 1, over[1], over[0]) - v[s])
+        for s in range(SB)
+    ]
+    under = [lroll(x, E)[:, 0:W] for x in f]
+    code = [CODE[3, s, 0:E, 0:W] for s in range(SB)]
+    for s in range(SB):
+        u = jnp.where(code[s] == 1, under[1], jnp.where(code[s] == 0, under[0], 0.0))
+        div[s] = div[s] + (f[s][:, 0:W] - u)
+    v = [x[0:E, 0:W] for x in upd]
+    last, first = zw == E - 1, zw == 0
+    up = [jnp.where(last, lroll(v[1], E - 1), lroll(v[0], -1)), lroll(v[1], -1)]
+    f = [LZ[s, 0:E, 0:W] * (up[s] - v[s]) for s in range(SB)]
+    under = [
+        jnp.where(first, 0.0, lroll(f[0], 1)),
+        jnp.where(first, lroll(f[0], 1 - E), lroll(f[1], 1)),
+    ]
+    for s in range(SB):
+        r = R[s, 0:E, 0:W] - (v[s] - div[s] - (f[s] - under[s]))
+        TO[s] = sol[s] + (coef[1][0][0:E, 0:W] * v[s] + coef[1][1][0:E, 0:W] * r)
 
     def x_face(b, side):
         shape = (8, W)
@@ -759,21 +803,22 @@
                 continue
             cid = nbr[b, OPP[p] - 1]
             if cy:
-                corner = CR[CORNER_OF[p], slot(cid, base_of(df, -cy), FB)]
-                corner = lroll(jnp.broadcast_to(corner, (8, H)), 4 * E)
+                which = jnp.full((8, H), slot(cid, base_of(df, -cy), FB))
+                first, second, third = corner_rows(CORNER_OF[p])
+                corner = jnp.where(which == 1, second, first)
+                corner = jnp.where(which == 2, third, corner)
                 corner = jnp.concatenate([corner, corner], axis=1)
                 edge = l8 < E if cy > 0 else l8 >= W - E
-                cand = jnp.where(edge, corner, lroll(a, E * cy))
+                cand = jnp.where(edge, corner, a)
             else:
-                other = XR[side, slot(cid, bf, FB)]
                 edge = z8 == 0 if cz > 0 else z8 == E - 1
-                cand = jnp.where(edge, lroll(other, -(E - 1) * cz), lroll(a, cz))
+                cand = jnp.where(edge, XR[side, slot(cid, bf, FB)], a)
             val = jnp.where(r8 == r, cand, val)
             ids = jnp.where((r8 == r) & edge, jnp.full(shape, cid), ids)
-        fall = XS[1 - side, b]
+        fall = FX[1 - side, b]
         wid = wall[b, dirn - 1]
         row = 7 if side == 0 else 0
-        tw = XER[side, slot(wid, bf, SB), row : row + 1, :]
+        tw = XR[side, FB + slot(wid, bf, SB), row : row + 1, :]
         hot = (r8 == HEAT) & (jnp.full(shape, wid) >= 0)
         fall = jnp.where(hot, 2.0 * tw - fall, fall)
         return jnp.where(ids >= 0, val, fall)
@@ -792,17 +837,14 @@
             if r == 0:
                 continue
             if cx:
-                val = jnp.where(group == r, rroll(a, cx), val)
                 continue
             cid = nbr[b, OPP[p] - 1]
-            other = YR[side, slot(cid, bf, FB)]
-            edge = zh == 0 if cz > 0 else zh == E - 1
-            cand = jnp.where(edge, lroll(other, -(E - 1) * cz), lroll(a, cz))
-            val = jnp.where(group == r, cand, val)
-            ids = jnp.where((group == r) & edge, jnp.full(shape, cid), ids)
-        fall = YS[1 - side, b]
+            edge = (group == r) & (zh == 0 if cz > 0 else zh == E - 1)
+            val = jnp.where(edge, YR[side, slot(cid, bf, FB)], val)
+            ids = jnp.where(edge, jnp.full(shape, cid), ids)
+        fall = FY[1 - side, b]
         wid = wall[b, dirn - 1]
-        tw = YER[side, slot(wid, bf, SB)]
+        tw = YR[side, FB + slot(wid, bf, SB)]
         tw = lroll(tw, -2 * E if side == 0 else HEAT * E)
         hot = (group == HEAT) & (jnp.full(shape, wid) >= 0)
         fall = jnp.where(hot, 2.0 * tw - fall, fall)
@@ -867,16 +909,13 @@
             pltpu.VMEM((SB, E, W), jnp.int32),
             vm(SB, E, W),
             vm(2, FB, 8, W),
-            vm(2, FB, 8, W),
             vm(2, FB, E, H),
-            vm(2, FB, E, H),
-            vm(4, FB, 1, H),
-            vm(4, FB, 1, H),
-            vm(2, SB, 8, W),
-            vm(2, SB, 8, W),
-            vm(2, SB, E, H),
-            vm(2, SB, E, H),
-            vm(4, SB, 8, H),
+            vm(2, FB + SB, 8, W),
+            vm(2, FB + SB, 8, W),
+            vm(2, FB + SB, E, H),
+            vm(2, FB + SB, E, H),
+            vm(4, 1 + SB, 8, H),
+            vm(4, 1 + SB, 8, H),
         ]
         + [vm(SB, EX, EL)] * 9
         + [
@@ -886,7 +925,7 @@
             pltpu.SMEM(wall.shape, jnp.int32),
             pltpu.SMEM(snbr.shape, jnp.int32),
             pltpu.SMEM(sflu.shape, jnp.int32),
-            pltpu.SemaphoreType.DMA((13,)),
+            pltpu.SemaphoreType.DMA((9,)),
             pltpu.SemaphoreType.DMA((N_COPY,)),
             pltpu.SemaphoreType.DMA((N_COPY,)),
         ],

time: 12.5 us -> 11.5 us (0.920)
  Pallas kernels: 11.7 us -> 10.6 us
    pallas_call x1, Pallas kernels: 10.6 us -> 9.55 us  [body(): pl.pallas_call(functools.partial(kernel, nf, nc), out_shape=(vm(FB, 19, E...]
where the time goes in v5:
time: 11.5 us; the launch traced here: 11.3 us
  Pallas kernels  10.6 us (92%)
  between operations  0.64 us (6%)
    pallas_call x1, Pallas kernels, body(): pl.pallas_call(functools.partial(kernel, nf, nc), out_shape=(vm(FB, 19, E...  9.55 us
    pallas_call x1, Pallas kernels, body(): pl.pallas_call(store_kernel, out_shape=(jax.ShapeDtypeStruct(fluid_pop.sh...  1.09 us

profile of v5, /device:TPU:24, one launch (start us, length us, event | category | flops | bytes accessed | tf_op | source)
XLA Modules:
  0.0 11.3 jit_solution(15344183708825414486)
XLA Ops:
  0.6 9.5 %shard_map.112 = (f32[3,19,16,256]{3,2,1,0:T(8,128)S(1)}, f32[3,7,16,256]{3,2,1,0:T(8,128)S(1)}, f32[2,16,256]{2,1,0:T(8,128)S(1)}) custom-call(f32[3,19,4096]{2,1,0:T(8,128)} %fluid_in.1, f32[3,7,4096]{2,1,0:T(8,128)} %heat_in.1, f32[2,4096]{1,0:T(2,128)} %temp_in.1, s32[2,4096]{1,0:T(2,128)} %mat_in.1, f32[8]{0:T(128)} %cond_in.1, s32[3,18]{1,0:T(4,128)} %nbr_in.1, ...), custom_call_target="tpu_custom_call" | custom-call | tf_op jit(solution)/shard_map/pallas_call | solution.py:896
  10.2 1.1 %shard_map.113 = (f32[3,19,4096]{2,1,0:T(8,128)}, f32[3,7,4096]{2,1,0:T(8,128)}, f32[2,4096]{1,0:T(2,128)}) custom-call(f32[3,19,16,256]{3,2,1,0:T(8,128)S(1)} %get-tuple-element.6.fluid, f32[3,7,16,256]{3,2,1,0:T(8,128)S(1)} %get-tuple-element.7.heat, f32[2,16,256]{2,1,0:T(8,128)S(1)} %get-tuple-element.8.solid), custom_call_target="tpu_custom_call" | custom-call | tf_op jit(solution)/shard_map/pallas_call | solution.py:936

commit v6 on v5

--- a/solution.py
+++ b/solution.py
@@ -457,8 +457,50 @@
     def piece(flag, v):
         return jnp.where(on(flag, v), v, 0.0)
 
-    with jax.named_scope("wait_faces"):
-        for i in range(8):
+    with jax.named_scope("wait_y"):
+        for i in (2, 3):
+            received(i)
+
+    def y_face(b, side):
+        shape = (E, H)
+        dc = -1 if side == 0 else 1
+        dirn = 4 if side == 0 else 3
+        bf = base_of(0, dc)
+        main_id = nbr[b, dirn - 1]
+        a = YR[side, slot(main_id, bf, FB)]
+        val = a
+        ids = jnp.full(shape, main_id)
+        for r, p in enumerate(PY[side]):
+            cx, _, cz = C[p]
+            if r == 0:
+                continue
+            if cx:
+                continue
+            cid = nbr[b, OPP[p] - 1]
+            edge = (group == r) & (zh == 0 if cz > 0 else zh == E - 1)
+            val = jnp.where(edge, YR[side, slot(cid, bf, FB)], val)
+            ids = jnp.where(edge, jnp.full(shape, cid), ids)
+        fall = FY[1 - side, b]
+        wid = wall[b, dirn - 1]
+        tw = YR[side, FB + slot(wid, bf, SB)]
+        tw = lroll(tw, -2 * E if side == 0 else HEAT * E)
+        hot = (group == HEAT) & (jnp.full(shape, wid) >= 0)
+        fall = jnp.where(hot, 2.0 * tw - fall, fall)
+        return jnp.where(ids >= 0, val, fall)
+
+    for b in range(FB):
+        for side in range(2):
+            yf = y_face(b, side)
+            half = pl.ds(0, H) if side == 0 else pl.ds(H, H)
+            edge = lh < E if side == 0 else lh >= H - E
+            back = 0 if side == 0 else H - E
+            for q, p in enumerate(PY[side]):
+                v = lroll(yf, back - E * q)
+                GO[b, p, :, half] = jnp.where(edge, v, GO[b, p, :, half])
+            v = lroll(yf, back - E * HEAT)
+            QO[b, 3 + side, :, half] = jnp.where(edge, v, QO[b, 3 + side, :, half])
+    with jax.named_scope("wait_x"):
+        for i in (0, 1, 4, 5, 6, 7):
             received(i)
 
     def corner_z(i):
@@ -823,44 +865,7 @@
         fall = jnp.where(hot, 2.0 * tw - fall, fall)
         return jnp.where(ids >= 0, val, fall)
 
-    def y_face(b, side):
-        shape = (E, H)
-        dc = -1 if side == 0 else 1
-        dirn = 4 if side == 0 else 3
-        bf = base_of(0, dc)
-        main_id = nbr[b, dirn - 1]
-        a = YR[side, slot(main_id, bf, FB)]
-        val = a
-        ids = jnp.full(shape, main_id)
-        for r, p in enumerate(PY[side]):
-            cx, _, cz = C[p]
-            if r == 0:
-                continue
-            if cx:
-                continue
-            cid = nbr[b, OPP[p] - 1]
-            edge = (group == r) & (zh == 0 if cz > 0 else zh == E - 1)
-            val = jnp.where(edge, YR[side, slot(cid, bf, FB)], val)
-            ids = jnp.where(edge, jnp.full(shape, cid), ids)
-        fall = FY[1 - side, b]
-        wid = wall[b, dirn - 1]
-        tw = YR[side, FB + slot(wid, bf, SB)]
-        tw = lroll(tw, -2 * E if side == 0 else HEAT * E)
-        hot = (group == HEAT) & (jnp.full(shape, wid) >= 0)
-        fall = jnp.where(hot, 2.0 * tw - fall, fall)
-        return jnp.where(ids >= 0, val, fall)
-
     for b in range(FB):
-        for side in range(2):
-            yf = y_face(b, side)
-            half = pl.ds(0, H) if side == 0 else pl.ds(H, H)
-            edge = lh < E if side == 0 else lh >= H - E
-            back = 0 if side == 0 else H - E
-            for q, p in enumerate(PY[side]):
-                v = lroll(yf, back - E * q)
-                GO[b, p, :, half] = jnp.where(edge, v, GO[b, p, :, half])
-            v = lroll(yf, back - E * HEAT)
-            QO[b, 3 + side, :, half] = jnp.where(edge, v, QO[b, 3 + side, :, half])
         for side in range(2):
             xf = x_face(b, side)
             x = 0 if side == 0 else E - 1

time: 11.5 us -> 11.3 us (0.983)
  Pallas kernels: 10.6 us -> 10.4 us
    pallas_call x1, Pallas kernels: 9.55 us -> 9.35 us  [body(): pl.pallas_call(functools.partial(kernel, nf, nc), out_shape=(vm(FB, 19, E...]
where the time goes in v6:
time: 11.3 us; the launch traced here: 11.1 us
  Pallas kernels  10.4 us (92%)
  between operations  0.64 us (6%)
    pallas_call x1, Pallas kernels, body(): pl.pallas_call(functools.partial(kernel, nf, nc), out_shape=(vm(FB, 19, E...  9.35 us
    pallas_call x1, Pallas kernels, body(): pl.pallas_call(store_kernel, out_shape=(jax.ShapeDtypeStruct(fluid_pop.sh...  1.09 us

profile of v6, /device:TPU:24, one launch (start us, length us, event | category | flops | bytes accessed | tf_op | source)
XLA Modules:
  0.0 11.1 jit_solution(8780999368291448532)
XLA Ops:
  0.6 9.4 %shard_map.112 = (f32[3,19,16,256]{3,2,1,0:T(8,128)S(1)}, f32[3,7,16,256]{3,2,1,0:T(8,128)S(1)}, f32[2,16,256]{2,1,0:T(8,128)S(1)}) custom-call(f32[3,19,4096]{2,1,0:T(8,128)} %fluid_in.1, f32[3,7,4096]{2,1,0:T(8,128)} %heat_in.1, f32[2,4096]{1,0:T(2,128)} %temp_in.1, s32[2,4096]{1,0:T(2,128)} %mat_in.1, f32[8]{0:T(128)} %cond_in.1, s32[3,18]{1,0:T(4,128)} %nbr_in.1, ...), custom_call_target="tpu_custom_call" | custom-call | tf_op jit(solution)/shard_map/pallas_call | solution.py:901
  10.0 1.1 %shard_map.113 = (f32[3,19,4096]{2,1,0:T(8,128)}, f32[3,7,4096]{2,1,0:T(8,128)}, f32[2,4096]{1,0:T(2,128)}) custom-call(f32[3,19,16,256]{3,2,1,0:T(8,128)S(1)} %get-tuple-element.6.fluid, f32[3,7,16,256]{3,2,1,0:T(8,128)S(1)} %get-tuple-element.7.heat, f32[2,16,256]{2,1,0:T(8,128)S(1)} %get-tuple-element.8.solid), custom_call_target="tpu_custom_call" | custom-call | tf_op jit(solution)/shard_map/pallas_call | solution.py:941

commit v7 on v6

--- a/solution.py
+++ b/solution.py
@@ -79,17 +79,18 @@
         return G[b, p, rs, ls]
 
     f = [ld(p) for p in range(19)]
+    w = [v * (1.0 / 3.0 if p == 0 else 1.0 / 18.0 if p < 7 else 1.0 / 36.0) for p, v in enumerate(f)]
     d = [None] * 19
     for p in (1, 3, 5, 7, 9, 11, 13, 15, 17):
-        d[p] = f[p] - f[p + 1]
-    s1 = ((f[1] + f[2]) + (f[3] + f[4])) + (f[5] + f[6])
-    s2 = (((f[7] + f[8]) + (f[9] + f[10])) + ((f[11] + f[12]) + (f[13] + f[14]))) + (
-        (f[15] + f[16]) + (f[17] + f[18])
+        d[p] = w[p] - w[p + 1]
+    s1 = ((w[1] + w[2]) + (w[3] + w[4])) + (w[5] + w[6])
+    s2 = (((w[7] + w[8]) + (w[9] + w[10])) + ((w[11] + w[12]) + (w[13] + w[14]))) + (
+        (w[15] + w[16]) + (w[17] + w[18])
     )
-    rho = f[0] * (1.0 / 3.0) + s1 * (1.0 / 18.0) + s2 * (1.0 / 36.0)
-    jx = d[1] * (1.0 / 18.0) + ((d[7] + d[9]) + (d[11] + d[13])) * (1.0 / 36.0)
-    jy = d[3] * (1.0 / 18.0) + ((d[7] - d[9]) + (d[15] + d[17])) * (1.0 / 36.0)
-    jz = d[5] * (1.0 / 18.0) + ((d[11] - d[13]) + (d[15] - d[17])) * (1.0 / 36.0)
+    rho = (w[0] + s1) + s2
+    jx = d[1] + ((d[7] + d[9]) + (d[11] + d[13]))
+    jy = d[3] + ((d[7] - d[9]) + (d[15] + d[17]))
+    jz = d[5] + ((d[11] - d[13]) + (d[15] - d[17]))
     inv = 1.0 / rho
     u = (jx * inv, jy * inv, jz * inv)
     j = (jx, jy, jz)
@@ -115,8 +116,9 @@
         G[b, p + 1, rs, ls] = (even - odd) - 0.25 * f[p + 1]
         cus[p] = cu
     h = [Q[b, k, rs, ls] for k in range(7)]
-    hs = ((h[1] + h[2]) + (h[3] + h[4])) + (h[5] + h[6])
-    t11 = (h[0] * 0.25 + hs * 0.125) * 1.1
+    g = [v * (0.25 if k == 0 else 0.125) for k, v in enumerate(h)]
+    gs = ((g[1] + g[2]) + (g[3] + g[4])) + (g[5] + g[6])
+    t11 = (g[0] + gs) * 1.1
     t44 = 4.0 * t11
     Q[b, 0, rs, ls] = t11 - 0.1 * h[0]
     for k in (1, 3, 5):
@@ -413,7 +415,7 @@
         pl.semaphore_wait(barrier, n_peers)
     for i, (df, dc) in enumerate(CORNERS):
         send(4 + i, CS.at[i], CR.at[i], df, dc)
-    for i, (df, dc) in enumerate(SIDES):
+    for i, (df, dc) in list(enumerate(SIDES))[::-1]:
         side = i % 2
         if i < 2:
             send(i, XS.at[side], XR.at[side], df, dc)

time: 11.3 us -> 11.3 us (level)
  no operation moved by 1% of the time
where the time goes in v7:
time: 11.3 us; the launch traced here: 11.1 us
  Pallas kernels  10.4 us (92%)
  between operations  0.64 us (6%)
    pallas_call x1, Pallas kernels, body(): pl.pallas_call(functools.partial(kernel, nf, nc), out_shape=(vm(FB, 19, E...  9.35 us
    pallas_call x1, Pallas kernels, body(): pl.pallas_call(store_kernel, out_shape=(jax.ShapeDtypeStruct(fluid_pop.sh...  1.09 us

profile of v7, /device:TPU:24, one launch (start us, length us, event | category | flops | bytes accessed | tf_op | source)
XLA Modules:
  0.0 11.1 jit_solution(14138697528854148716)
XLA Ops:
  0.6 9.4 %shard_map.112 = (f32[3,19,16,256]{3,2,1,0:T(8,128)S(1)}, f32[3,7,16,256]{3,2,1,0:T(8,128)S(1)}, f32[2,16,256]{2,1,0:T(8,128)S(1)}) custom-call(f32[3,19,4096]{2,1,0:T(8,128)} %fluid_in.1, f32[3,7,4096]{2,1,0:T(8,128)} %heat_in.1, f32[2,4096]{1,0:T(2,128)} %temp_in.1, s32[2,4096]{1,0:T(2,128)} %mat_in.1, f32[8]{0:T(128)} %cond_in.1, s32[3,18]{1,0:T(4,128)} %nbr_in.1, ...), custom_call_target="tpu_custom_call" | custom-call | tf_op jit(solution)/shard_map/pallas_call | solution.py:903
  10.0 1.1 %shard_map.113 = (f32[3,19,4096]{2,1,0:T(8,128)}, f32[3,7,4096]{2,1,0:T(8,128)}, f32[2,4096]{1,0:T(2,128)}) custom-call(f32[3,19,16,256]{3,2,1,0:T(8,128)S(1)} %get-tuple-element.6.fluid, f32[3,7,16,256]{3,2,1,0:T(8,128)S(1)} %get-tuple-element.7.heat, f32[2,16,256]{2,1,0:T(8,128)S(1)} %get-tuple-element.8.solid), custom_call_target="tpu_custom_call" | custom-call | tf_op jit(solution)/shard_map/pallas_call | solution.py:943

commit v8 on v7

--- a/solution.py
+++ b/solution.py
@@ -459,6 +459,27 @@
     def piece(flag, v):
         return jnp.where(on(flag, v), v, 0.0)
 
+    kmax = cond[0]
+    for i in range(1, 8):
+        kmax = jnp.maximum(kmax, cond[i])
+    radius = jnp.full((8, H), kmax * 6.0, F32)
+    center = radius + 1.0
+    sigma = center / radius
+
+    def grow(v):
+        v = jnp.concatenate([v] * (EX // 8), axis=0)
+        return jnp.concatenate([v] * (EL // H), axis=1)
+
+    inv_center = grow(1.0 / center)
+    rho0 = 1.0 / sigma
+    rho1 = 1.0 / (2.0 * sigma - rho0)
+    rho2 = 1.0 / (2.0 * sigma - rho1)
+    coef = [
+        (grow(rho1 * rho0), grow(2.0 * rho1 / radius)),
+        (grow(rho2 * rho1), grow(2.0 * rho2 / radius)),
+    ]
+
+
     with jax.named_scope("wait_y"):
         for i in (2, 3):
             received(i)
@@ -550,7 +571,11 @@
         Z.append(jnp.concatenate([top, low], axis=0))
 
     def link(k, kb):
-        return (2.0 * k * kb) / jnp.maximum(k + kb, 0.05)
+        total = jnp.maximum(k + kb, 0.05)
+        inv = pl.reciprocal(total, approx=True)
+        inv = inv * (2.0 - total * inv)
+        inv = inv * (2.0 - total * inv)
+        return (2.0 * k * kb) * inv
 
     def toward(k, v):
         return rroll(v, -1 if k == 0 else 1) if k < 2 else lroll(v, -E if k == 2 else E)
@@ -611,27 +636,6 @@
     div = divergence(tt)
     for s in range(SB):
         R[s] = div[s] - (WX[s] + WY[s] + WZ[s]) * tt[s]
-
-    kmax = cond[0]
-    for i in range(1, 8):
-        kmax = jnp.maximum(kmax, cond[i])
-    radius = jnp.full((8, H), kmax * 6.0, F32)
-    center = radius + 1.0
-    sigma = center / radius
-
-    def grow(v):
-        v = jnp.concatenate([v] * (EX // 8), axis=0)
-        return jnp.concatenate([v] * (EL // H), axis=1)
-
-    inv_center = grow(1.0 / center)
-    rho0 = 1.0 / sigma
-    rho1 = 1.0 / (2.0 * sigma - rho0)
-    rho2 = 1.0 / (2.0 * sigma - rho1)
-    coef = [
-        (grow(rho1 * rho0), grow(2.0 * rho1 / radius)),
-        (grow(rho2 * rho1), grow(2.0 * rho2 / radius)),
-    ]
-
 
     def corner_rows(i):
         return [jnp.broadcast_to(CR[i, 0, j : j + 1, :], (8, H)) for j in range(FB)]

time: 11.3 us -> 11.3 us (level)
  no operation moved by 1% of the time
where the time goes in v8:
time: 11.3 us; the launch traced here: 11.1 us
  Pallas kernels  10.5 us (93%)
  between operations  0.64 us (6%)
    pallas_call x1, Pallas kernels, body(): pl.pallas_call(functools.partial(kernel, nf, nc), out_shape=(vm(FB, 19, E...  9.39 us
    pallas_call x1, Pallas kernels, body(): pl.pallas_call(store_kernel, out_shape=(jax.ShapeDtypeStruct(fluid_pop.sh...  1.09 us

profile of v8, /device:TPU:24, one launch (start us, length us, event | category | flops | bytes accessed | tf_op | source)
XLA Modules:
  0.0 11.1 jit_solution(15466813336490120139)
XLA Ops:
  0.6 9.4 %shard_map.112 = (f32[3,19,16,256]{3,2,1,0:T(8,128)S(1)}, f32[3,7,16,256]{3,2,1,0:T(8,128)S(1)}, f32[2,16,256]{2,1,0:T(8,128)S(1)}) custom-call(f32[3,19,4096]{2,1,0:T(8,128)} %fluid_in.1, f32[3,7,4096]{2,1,0:T(8,128)} %heat_in.1, f32[2,4096]{1,0:T(2,128)} %temp_in.1, s32[2,4096]{1,0:T(2,128)} %mat_in.1, f32[8]{0:T(128)} %cond_in.1, s32[3,18]{1,0:T(4,128)} %nbr_in.1, ...), custom_call_target="tpu_custom_call" | custom-call | tf_op jit(solution)/shard_map/pallas_call | solution.py:907
  10.0 1.1 %shard_map.113 = (f32[3,19,4096]{2,1,0:T(8,128)}, f32[3,7,4096]{2,1,0:T(8,128)}, f32[2,4096]{1,0:T(2,128)}) custom-call(f32[3,19,16,256]{3,2,1,0:T(8,128)S(1)} %get-tuple-element.6.fluid, f32[3,7,16,256]{3,2,1,0:T(8,128)S(1)} %get-tuple-element.7.heat, f32[2,16,256]{2,1,0:T(8,128)S(1)} %get-tuple-element.8.solid), custom_call_target="tpu_custom_call" | custom-call | tf_op jit(solution)/shard_map/pallas_call | solution.py:947

commit v9 on v7

--- a/solution.py
+++ b/solution.py
@@ -297,9 +297,8 @@
         nbr_has.append(has)
         nbr_z.append((jnp.where(has > 0, za, NONE), jnp.where(has > 0, zb, NONE)))
 
-    with jax.named_scope("wait_solid"):
-        all_of(T, in_sem.at[0]).wait()
-        all_of(M, in_sem.at[1]).wait()
+    all_of(T, in_sem.at[0]).wait()
+    all_of(M, in_sem.at[1]).wait()
     for s in range(SB):
         m = M[s]
         k = jnp.full(wide, cond[0], F32)
@@ -330,14 +329,12 @@
     def two(v, first, second, z):
         return jnp.where((z == 0) | (z == E - 1), v, jnp.where(z < 8, first, second))
 
-    with jax.named_scope("wait_pops"):
-        all_of(G, in_sem.at[2]).wait()
-        all_of(Q, in_sem.at[3]).wait()
+    all_of(G, in_sem.at[2]).wait()
+    all_of(Q, in_sem.at[3]).wait()
     for b in range(FB):
-        with jax.named_scope("collide"):
-            for xh in range(2):
-                for yh in range(2):
-                    collide_tile(G, Q, b, pl.ds(8 * xh, 8), pl.ds(H * yh, H))
+        for xh in range(2):
+            for yh in range(2):
+                collide_tile(G, Q, b, pl.ds(8 * xh, 8), pl.ds(H * yh, H))
         for side in range(2):
             x = E - 1 if side == 0 else 0
             inner = E - 2 if side == 0 else 1
@@ -411,8 +408,7 @@
         for s in range(SB):
             CS[i, 1 + s] = XS[side, FB + s, :, H * ch : H * ch + H]
 
-    with jax.named_scope("entry_barrier"):
-        pl.semaphore_wait(barrier, n_peers)
+    pl.semaphore_wait(barrier, n_peers)
     for i, (df, dc) in enumerate(CORNERS):
         send(4 + i, CS.at[i], CR.at[i], df, dc)
     for i, (df, dc) in list(enumerate(SIDES))[::-1]:
@@ -449,9 +445,8 @@
         for p in range(1, 7):
             QO[b, p] = main(Q, p)
 
-    with jax.named_scope("stream"):
-        for b in range(FB):
-            stream(b)
+    for b in range(FB):
+        stream(b)
 
     ext = (EX, EL)
     ze = jnp.bitwise_and(lanes(ext), E - 1)
@@ -459,9 +454,8 @@
     def piece(flag, v):
         return jnp.where(on(flag, v), v, 0.0)
 
-    with jax.named_scope("wait_y"):
-        for i in (2, 3):
-            received(i)
+    for i in (2, 3):
+        received(i)
 
     def y_face(b, side):
         shape = (E, H)
@@ -501,9 +495,8 @@
                 GO[b, p, :, half] = jnp.where(edge, v, GO[b, p, :, half])
             v = lroll(yf, back - E * HEAT)
             QO[b, 3 + side, :, half] = jnp.where(edge, v, QO[b, 3 + side, :, half])
-    with jax.named_scope("wait_x"):
-        for i in (0, 1, 4, 5, 6, 7):
-            received(i)
+    for i in (0, 1, 4, 5, 6, 7):
+        received(i)
 
     def corner_z(i):
         side = CORNER_SRC[i][0]
@@ -888,7 +881,7 @@
         for x in range(E):
             pltpu.make_async_copy(
                 src.at[..., x, :], dst.at[..., pl.ds(W * x, W)], sem.at[i]
-            ).start()
+            ).start(priority=x % 2)
     for i, (src, dst) in enumerate(pairs):
         pltpu.make_async_copy(src, src, sem.at[i]).wait()
 

time: 11.3 us -> 11.3 us (level)
  no operation moved by 1% of the time
where the time goes in v9:
time: 11.3 us; the launch traced here: 11.1 us
  Pallas kernels  10.4 us (92%)
  between operations  0.64 us (6%)
    pallas_call x1, Pallas kernels, body(): pl.pallas_call(functools.partial(kernel, nf, nc), out_shape=(vm(FB, 19, E...  9.36 us
    pallas_call x1, Pallas kernels, body(): pl.pallas_call(store_kernel, out_shape=(jax.ShapeDtypeStruct(fluid_pop.sh...  1.09 us

profile of v9, /device:TPU:24, one launch (start us, length us, event | category | flops | bytes accessed | tf_op | source)
XLA Modules:
  0.0 11.1 jit_solution(14138697528854148716)
XLA Ops:
  0.6 9.4 %shard_map.112 = (f32[3,19,16,256]{3,2,1,0:T(8,128)S(1)}, f32[3,7,16,256]{3,2,1,0:T(8,128)S(1)}, f32[2,16,256]{2,1,0:T(8,128)S(1)}) custom-call(f32[3,19,4096]{2,1,0:T(8,128)} %fluid_in.1, f32[3,7,4096]{2,1,0:T(8,128)} %heat_in.1, f32[2,4096]{1,0:T(2,128)} %temp_in.1, s32[2,4096]{1,0:T(2,128)} %mat_in.1, f32[8]{0:T(128)} %cond_in.1, s32[3,18]{1,0:T(4,128)} %nbr_in.1, ...), custom_call_target="tpu_custom_call" | custom-call | tf_op jit(solution)/shard_map/pallas_call | solution.py:896
  10.0 1.1 %shard_map.113 = (f32[3,19,4096]{2,1,0:T(8,128)}, f32[3,7,4096]{2,1,0:T(8,128)}, f32[2,4096]{1,0:T(2,128)}) custom-call(f32[3,19,16,256]{3,2,1,0:T(8,128)S(1)} %get-tuple-element.6.fluid, f32[3,7,16,256]{3,2,1,0:T(8,128)S(1)} %get-tuple-element.7.heat, f32[2,16,256]{2,1,0:T(8,128)S(1)} %get-tuple-element.8.solid), custom_call_target="tpu_custom_call" | custom-call | tf_op jit(solution)/shard_map/pallas_call | solution.py:936
